TPU v7x, 32 devices: a whole 2x2x4 slice. The times are simulated.
32 devices in a mesh: seq: 8 (over z, y), rep: 4 (over x, core).
Axes of the slice: x: 2, y: 2, z: 4, core: 2. Of those that a mesh axis runs over, the one named last changes fastest.
Arguments:
- inputs: bfloat16 [64, 512, 512], P('rep', 'seq'), may hold values from -6 to 6
- cotangent: bfloat16 [64, 512, 512], P('rep', 'seq'), may hold values from -6 to 6
- segments: int32 [64, 512], P('rep', 'seq'), may hold values from 0 to 511, as said below
- owners: int32 [24], replicated, may hold values from 0 to 23, each once
- weights: float32 [512, 24, 256], P('seq', 'rep'), may hold values from -0.25 to 0.25
- left_bases: float32 [24, 512, 512], P('rep'), as said below
- right_bases: float32 [24, 256, 256], P('rep'), as said below
- moment_one: float32 [512, 24, 256], P('seq', 'rep')
- moment_two: float32 [512, 24, 256], P('seq', 'rep'), as said below
- norm_params: float32 [4, 512], replicated
- norm_one: float32 [4, 512], replicated
- norm_two: float32 [4, 512], replicated, as said below
- positions: float32 [512, 512], replicated, may hold values from -3 to 3
- pos_one: float32 [512, 512], replicated
- pos_two: float32 [512, 512], replicated, as said below
Outputs:
- result: bfloat16 [64, 512, 512], P('rep', 'seq')
- input_grad: float32 [64, 512, 512], P('rep', 'seq')
- new_moment_one: float32 [512, 24, 256], P('seq', 'rep')
- new_moment_two: float32 [512, 24, 256], P('seq', 'rep')
- new_weights: float32 [512, 24, 256], P('seq', 'rep')
- new_norm_one: float32 [4, 512], replicated
- new_norm_two: float32 [4, 512], replicated
- new_norms: float32 [4, 512], replicated
- new_pos_one: float32 [512, 512], replicated
- new_pos_two: float32 [512, 512], replicated
- new_positions: float32 [512, 512], replicated
Inputs may be any that keep to these rules, and one draw needn't show every extreme that they name: `segments`: each row starts at document 0 and its numbers never fall, by at most one from a character to the next; in each aligned block of 16 rows one row is a single document and another has a new document at every character. `owners`: each slot holds exactly one tile. `left_bases`: each slot's basis is orthogonal. `right_bases`: each slot's basis is orthogonal. `moment_two`: all entries are positive. `norm_two`: all entries are positive. `pos_two`: all entries are positive.
All inputs are finite; a program needn't handle non-finite values.
Results may differ from a plain program's by a relative error of at most 0.015.
Values may be sent and summed in bfloat16 or wider, within the bound.
No kernel may reach another device: no remote copies, remote signals or barrier semaphores. Data moves between devices by JAX's collectives and lax.ppermute only.
A program may use at most 192 MiB of HBM per device.

v0:
```python
import functools

import jax
import jax.numpy as jnp
import numpy as np
from jax import lax
from jax.experimental import pallas as pl
from jax.experimental.pallas import tpu as pltpu
from jax.sharding import PartitionSpec as P

H = 8
WIN = 512
STEP = 10

EPS_NORM = 1e-05
EPS_ADAM = 1e-08
BETA = 0.5
LEARN = 0.02
LEARN_SMALL = 0.2
DECAY = 0.01
MASKED = -1e30
QUERIES = 128

BF = jnp.bfloat16
F32 = jnp.float32
PARAMS = pltpu.CompilerParams(vmem_limit_bytes=58 * 1024 * 1024)
GELU_A = 0.7978845608028654
GELU_B = 0.044715


def nn(a, b):
    return lax.dot_general(a, b, (((1,), (0,)), ((), ())), preferred_element_type=F32)


def nt(a, b):
    return lax.dot_general(a, b, (((1,), (1,)), ((), ())), preferred_element_type=F32)


def tn(a, b):
    return lax.dot_general(a, b, (((0,), (0,)), ((), ())), preferred_element_type=F32)


def adam_step(gradient, first, second):
    first_new = BETA * first + (1.0 - BETA) * gradient
    second_new = BETA * second + (1.0 - BETA) * gradient * gradient
    fix = 1.0 - BETA**STEP
    direction = first_new / fix / (jnp.sqrt(second_new / fix) + EPS_ADAM)
    return (first_new, second_new, direction)


def row_norm(values):
    center = values - jnp.mean(values, axis=-1, keepdims=True)
    inverse = lax.rsqrt(jnp.mean(center * center, axis=-1, keepdims=True) + EPS_NORM)
    return center * inverse, inverse


def norm_pull(grad_rows, scaled, inverse, gain):
    scaled_grad = grad_rows * gain
    grad_input = inverse * (
        scaled_grad
        - jnp.mean(scaled_grad, axis=-1, keepdims=True)
        - scaled * jnp.mean(scaled_grad * scaled, axis=-1, keepdims=True)
    )
    grad_gain = jnp.sum(grad_rows * scaled, axis=0, keepdims=True)
    grad_shift = jnp.sum(grad_rows, axis=0, keepdims=True)
    return grad_input, grad_gain, grad_shift


def memory(mebibytes):
    return pltpu.CompilerParams(vmem_limit_bytes=mebibytes * 1024 * 1024)


def same(shape):
    return pl.BlockSpec(shape, lambda *_: (0,) * len(shape), pipeline_mode=pl.Buffered(1))


def whole(shape):
    return pl.BlockSpec(shape, lambda *_: (0,) * len(shape))


SCALARS = pl.BlockSpec(memory_space=pltpu.SMEM)


def takes(microseconds):
    return pl.CostEstimate(flops=int(microseconds * 1e6), bytes_accessed=0, transcendentals=0)


def gather_masks(order):
    masks = [(0, 0)]
    for axis, bit in order:
        step = (bit, 0) if axis == "seq" else (0, bit)
        masks = masks + [(s ^ step[0], t ^ step[1]) for s, t in masks]
    return tuple(masks)


def beyond(masks):
    return tuple((s, t ^ 1) for s, t in masks)


def block_at(me_ref, mask, reps, rows):
    block = (me_ref[0] ^ mask[0]) * reps + (me_ref[1] ^ mask[1])
    return pl.ds(pl.multiple_of(block * rows, rows), rows)


def place_blocks(me_ref, refs, target, plans, reps):
    if plans is None:
        target[...] = refs[0][...]
        return
    for ref, (first, last, masks) in zip(refs, plans):
        for k, mask in enumerate(masks):
            where = block_at(me_ref, mask, reps, ref.shape[2])
            target[first:last, where, :] = ref[k, : last - first]


def take_blocks(me_ref, source, outs, plans, reps, rows):
    if plans is None:
        outs[0][...] = source[...].astype(BF)
        return
    for out, parts in zip(outs, plans):
        at = 0
        for first, last, masks in parts:
            for mask in masks:
                where = block_at(me_ref, mask, reps, rows)
                out[at : at + last - first] = source[first:last, where, :].astype(BF)
                at += last - first


def attend_kernel(plans, reps, me_ref, x_ref, pos_ref, ids_row, ids_col, *refs):
    count = 1 if plans is None else len(plans)
    pieces = refs[:count]
    qkv_ref, mixed_ref, lse_ref, bias, w_ref = refs[count:]
    win, width = pos_ref.shape
    dim = width // H
    tile = w_ref.shape[2]


    @pl.when(pl.program_id(0) == 0)
    def _():
        place_blocks(me_ref, pieces, w_ref, plans, reps)

    hidden = x_ref[...].reshape(win, width).astype(F32) + pos_ref[...]
    low = hidden.astype(BF)
    for t in range(w_ref.shape[0]):
        qkv_ref[0, :, t * tile : (t + 1) * tile] = nn(low, w_ref[t]).astype(BF)
    row = lax.broadcasted_iota(jnp.int32, (win, win), 0)
    col = lax.broadcasted_iota(jnp.int32, (win, win), 1)
    allowed = (ids_col[0] == ids_row[0]) & (col >= row)
    bias[...] = jnp.where(allowed, 0.0, MASKED)
    ones = jnp.ones((win, dim), BF)
    blocks = [(lo, lo + QUERIES) for lo in range(0, win, QUERIES)]

    def score(h):
        base = 3 * dim * h
        query = qkv_ref[0, :, base : base + dim] * (dim**-0.5)
        keys = qkv_ref[0, :, base + dim : base + 2 * dim]
        return [nt(keys[:hi], query[lo:hi]) + bias[:hi, lo:hi] for lo, hi in blocks]

    def mix(h, scores):
        base = 3 * dim * h
        values = jnp.concatenate([qkv_ref[0, :, base + 2 * dim : base + 3 * dim], ones], axis=1)
        values = values.T[: dim + 16]
        parts, logs = [], []
        for some in scores:
            highest = jnp.max(some, axis=0, keepdims=True)
            both = nn(values[:, : some.shape[0]], jnp.exp(some - highest).astype(BF))
            total = both[dim : dim + 1]
            parts.append(both[:dim] / total)
            logs.append(highest + jnp.log(total))
        lse_ref[0, h : h + 1] = jnp.concatenate(logs, axis=1)
        return jnp.concatenate(parts, axis=1).astype(BF)

    outs = []
    scores = score(0)
    for h in range(H):
        later = score(h + 1) if h + 1 < H else None
        outs.append(mix(h, scores))
        scores = later
    mixed_ref[0] = jnp.concatenate(outs, axis=0).T


def attend_forward(me, x, positions, ids, w, plans, tiles, tile, reps):
    group, wins, span, width = x.shape
    win = group * span
    return pl.pallas_call(
        functools.partial(attend_kernel, plans, reps),
        grid=(wins,),
        in_specs=[
            SCALARS,
            pl.BlockSpec((group, 1, span, width), lambda i: (0, i, 0, 0)),
            same((win, width)),
            pl.BlockSpec((1, 1, win), lambda i: (i, 0, 0)),
            pl.BlockSpec((1, win, 1), lambda i: (i, 0, 0)),
        ]
        + [same(piece.shape) for piece in w],
        out_specs=[
            pl.BlockSpec((1, win, 3 * width), lambda i: (i, 0, 0)),
            pl.BlockSpec((1, win, width), lambda i: (i, 0, 0)),
            pl.BlockSpec((1, H, win), lambda i: (i, 0, 0)),
        ],
        out_shape=[
            jax.ShapeDtypeStruct((wins, win, 3 * width), BF),
            jax.ShapeDtypeStruct((wins, win, width), BF),
            jax.ShapeDtypeStruct((wins, H, win), F32),
        ],
        scratch_shapes=[pltpu.VMEM((win, win), F32), pltpu.VMEM((tiles, width, tile), BF)],
        compiler_params=memory(32),
        cost_estimate=takes(18),
        name="attend_forward",
    )(me, x, positions, ids[:, None, :], ids[:, :, None], *w)


def middle_kernel(
    plans, out_plans, reps, rows, outs, wins, me_ref, x_ref, pos_ref, mixed_ref, cot_ref, norm_ref, moments_ref, *refs
):
    count = 1 if plans is None else len(plans)
    pieces = refs[:count]
    refs = refs[count:]
    result_ref, mid_ref, gmixed_ref, dnorm_ref = refs[:4]
    count = 1 if out_plans is None else 2
    grads = refs[4 : 4 + count]
    act, slope, gpre, w_ref, acc = refs[4 + count :]
    step = pl.program_id(0)
    last = wins - 1
    win, width = pos_ref.shape
    tile = w_ref.shape[2]
    ups = (w_ref.shape[0] - outs) // 2
    blocks = ups // 2
    up, down = outs, outs + ups

    @pl.when(step == 0)
    def _():
        place_blocks(me_ref, pieces, w_ref, plans, reps)
        acc[...] = jnp.zeros_like(acc)
        dnorm_ref[...] = jnp.zeros_like(dnorm_ref)
        if result_ref.shape[2] > (last + 1) * width:
            result_ref[:, :, (last + 1) * width :] = moments_ref[...]

    mixed = mixed_ref[0]
    hidden = x_ref[...].reshape(win, width).astype(F32) + pos_ref[...]
    attn = jnp.concatenate([nn(mixed, w_ref[t]) for t in range(outs)], axis=1)
    scaled_one, inverse_one = row_norm(hidden + attn)
    normed = scaled_one * norm_ref[0:1] + norm_ref[1:2]
    low = normed.astype(BF)
    for t in range(ups):
        pre = nn(low, w_ref[up + t])
        square = pre * pre
        bent = jnp.tanh(GELU_A * pre * (1.0 + GELU_B * square))
        act[:, t * tile : (t + 1) * tile] = (0.5 * pre * (1.0 + bent)).astype(BF)
        slope[:, t * tile : (t + 1) * tile] = (
            0.5 * (1.0 + bent)
            + 0.5 * pre * (1.0 - bent * bent) * (GELU_A + 3.0 * GELU_A * GELU_B * square)
        ).astype(BF)
    branch = jnp.concatenate(
        [
            sum(nn(act[:, b * width : (b + 1) * width], w_ref[down + 2 * b + j]) for b in range(blocks))
            for j in range(2)
        ],
        axis=1,
    )
    scaled_two, inverse_two = row_norm(normed + branch)
    result = scaled_two * norm_ref[2:3] + norm_ref[3:4]
    result = result.astype(BF).reshape(*result_ref.shape[:2], width)
    for window in range(wins):

        @pl.when(step == window)
        def _():
            result_ref[:, :, window * width : (window + 1) * width] = result

    grad_resid, gain_two, shift_two = norm_pull(
        cot_ref[...].reshape(win, width).astype(F32), scaled_two, inverse_two, norm_ref[2:3]
    )
    gb = grad_resid.astype(BF)
    for b in range(blocks):
        cols = slice(b * width, (b + 1) * width)
        gact = nt(gb[:, :tile], w_ref[down + 2 * b]) + nt(gb[:, tile:], w_ref[down + 2 * b + 1])
        gpre[:, cols] = (gact * slope[:, cols].astype(F32)).astype(BF)
    grad_normed = grad_resid + sum(
        nt(gpre[:, t * tile : (t + 1) * tile], w_ref[up + t]) for t in range(ups)
    )
    grad_mid, gain_one, shift_one = norm_pull(grad_normed, scaled_one, inverse_one, norm_ref[0:1])
    mid_ref[0] = grad_mid
    ga = grad_mid.astype(BF)
    gmixed_ref[0] = sum(nt(ga[:, t * tile : (t + 1) * tile], w_ref[t]) for t in range(outs)).astype(BF)
    dnorm_ref[...] += jnp.concatenate([gain_one, shift_one, gain_two, shift_two], axis=0)
    for b in range(blocks):
        act_t = act[:, b * width : (b + 1) * width].T
        for j in range(2):
            acc[down + 2 * b + j] += nn(act_t, gb[:, j * tile : (j + 1) * tile])
    low_t = low.T
    for t in range(ups):
        acc[up + t] += nn(low_t, gpre[:, t * tile : (t + 1) * tile])
    mixed_t = mixed.T
    for t in range(outs):
        acc[t] += nn(mixed_t, ga[:, t * tile : (t + 1) * tile])

    @pl.when(step == last)
    def _():
        take_blocks(me_ref, acc, grads, out_plans, reps, rows)


def middle(me, x, positions, mixed, cot, norms, moments, together, w, plans, out_plans, grad_shapes, tiles, tile, reps, rows):
    group, wins, span, width = x.shape
    win = group * span
    outs = width // tile
    hidden = (tiles - outs) // 2 * tile
    sent = (group, span, wins * width + (moments.shape[2] if together else 0))
    seq_spec = pl.BlockSpec((group, 1, span, width), lambda i: (0, i, 0, 0))
    row_spec = pl.BlockSpec((1, win, width), lambda i: (i, 0, 0))
    return pl.pallas_call(
        functools.partial(middle_kernel, plans, out_plans, reps, rows, outs, wins),
        grid=(wins,),
        in_specs=[
            SCALARS,
            seq_spec,
            same((win, width)),
            row_spec,
            seq_spec,
            same(norms.shape),
            same(moments.shape),
        ]
        + [same(piece.shape) for piece in w],
        out_specs=[whole(sent), row_spec, row_spec, whole(norms.shape)]
        + [whole(shape) for shape in grad_shapes],
        out_shape=[
            jax.ShapeDtypeStruct(sent, BF),
            jax.ShapeDtypeStruct((wins, win, width), F32),
            jax.ShapeDtypeStruct((wins, win, width), BF),
            jax.ShapeDtypeStruct(norms.shape, F32),
        ]
        + [jax.ShapeDtypeStruct(shape, BF) for shape in grad_shapes],
        scratch_shapes=[
            pltpu.VMEM((win, hidden), BF),
            pltpu.VMEM((win, hidden), BF),
            pltpu.VMEM((win, hidden), BF),
            pltpu.VMEM((tiles, width, tile), BF),
            pltpu.VMEM((tiles, width, tile), F32),
        ],
        compiler_params=PARAMS,
        cost_estimate=takes(27),
        name="middle",
    )(me, x, positions, mixed, cot, norms, moments, *w)


def attend_back_kernel(
    plans,
    out_plans,
    reps,
    rows,
    behind,
    me_ref,
    x_ref,
    pos_ref,
    ids_row,
    ids_col,
    qkv_ref,
    lse_ref,
    gmixed_ref,
    mid_ref,
    dnorm_ref,
    *refs,
):
    count = 1 if plans is None else len(plans)
    pieces = refs[:count]
    ginput_ref = refs[count + behind]
    refs = refs[count + behind + 1 :]
    count = 1 if out_plans is None else 2
    grads = refs[:count]
    bias, gproj, w_ref, acc = refs[count:]
    step = pl.program_id(0)
    last = pl.num_programs(0) - 1
    win, width = pos_ref.shape
    dim = width // H
    tiles, _, tile = w_ref.shape
    factor = dim**-0.5
    half = win // 2

    @pl.when(step == 0)
    def _():
        place_blocks(me_ref, pieces, w_ref, plans, reps)
        acc[...] = jnp.zeros_like(acc)

    key = lax.broadcasted_iota(jnp.int32, (win, win), 0)
    query_at = lax.broadcasted_iota(jnp.int32, (win, win), 1)
    allowed = (ids_col[0] == ids_row[0]) & (query_at >= key)
    bias[...] = jnp.where(allowed, 0.0, MASKED)
    blocks = [(lo, lo + QUERIES) for lo in range(0, win, QUERIES)]

    def operands(h):
        base = 3 * dim * h
        query = qkv_ref[0, :, base : base + dim] * factor
        keys = qkv_ref[0, :, base + dim : base + 2 * dim]
        values = qkv_ref[0, :, base + 2 * dim : base + 3 * dim]
        return query, keys, values, gmixed_ref[0, :, h * dim : (h + 1) * dim]

    def score(h):
        query, keys, values, gout = operands(h)
        return [
            (nt(keys[:hi], query[lo:hi]) + bias[:hi, lo:hi], nt(values[:hi], gout[lo:hi])) for lo, hi in blocks
        ]

    def pull(h, scores):
        query, keys, _, gout = operands(h)
        keys_t = jnp.concatenate([keys, keys], axis=1).T[:dim]
        probs, gscores, gqueries = [], [], []
        for (lo, hi), (some, gprobs) in zip(blocks, scores):
            weights = jnp.exp(some - lse_ref[0, h : h + 1, lo:hi])
            inner = jnp.sum(weights * gprobs, axis=0, keepdims=True)
            gscore = (weights * (gprobs - inner)).astype(BF)
            probs.append(weights.astype(BF))
            gscores.append(gscore)
            gqueries.append(nn(keys_t[:, :hi], gscore))
        gkeys, gvalues = [], []
        for lo, hi in blocks:
            later = [i for i, (_, end) in enumerate(blocks) if end >= hi]
            gkeys.append(nn(jnp.concatenate([gscores[i][lo:hi] for i in later], axis=1), query[lo:]))
            gvalues.append(nn(jnp.concatenate([probs[i][lo:hi] for i in later], axis=1), gout[lo:]))
        gquery = jnp.concatenate(gqueries, axis=1) * factor
        return gquery.astype(BF), [jnp.concatenate(part, axis=0).astype(BF) for part in (gkeys, gvalues)]

    done = []
    scores = score(0)
    for h in range(H):
        later = score(h + 1) if h + 1 < H else None
        done.append(pull(h, scores))
        scores = later
        if h % 2:
            packed = jnp.concatenate([done[-2][0], done[-1][0]], axis=0).T
            parts = [packed[:, :dim], *done[-2][1], packed[:, dim:], *done[-1][1]]
            gproj[:, 3 * dim * (h - 1) : 3 * dim * (h + 1)] = jnp.concatenate(parts, axis=1)
    hidden = x_ref[...].reshape(win, width).astype(F32) + pos_ref[...]
    low_t = hidden.astype(BF).T
    total = mid_ref[0]
    for t in range(tiles):
        part = gproj[:, t * tile : (t + 1) * tile]
        acc[t] += nn(low_t, part)
        total += nt(part, w_ref[t])
    ginput_ref[...] = total.astype(BF).reshape(ginput_ref.shape)
    for j in range(width // tile):
        acc[tiles + j] += total[:, j * tile : (j + 1) * tile]

    @pl.when(step == last)
    def _():
        if out_plans is not None:
            small = jnp.concatenate(
                [dnorm_ref[:, j * tile : (j + 1) * tile] for j in range(width // tile)], axis=0
            )
            small = jnp.concatenate([small, jnp.zeros((rows - small.shape[0], tile), F32)], axis=0)
            for b in range(win // rows):
                acc[acc.shape[0] - 1, b * rows : (b + 1) * rows] = small
        take_blocks(me_ref, acc, grads, out_plans, reps, rows)


def attend_backward(
    me, x, positions, ids, qkv, lse, gmixed, mid, dnorm, behind, w, plans, out_plans, grad_shapes, tiles, tile, reps, rows
):
    group, wins, span, width = x.shape
    win = group * span
    seq_spec = pl.BlockSpec((group, 1, span, width), lambda i: (0, i, 0, 0))
    row_spec = pl.BlockSpec((1, win, width), lambda i: (i, 0, 0))
    return pl.pallas_call(
        functools.partial(attend_back_kernel, plans, out_plans, reps, rows, len(behind)),
        grid=(wins,),
        in_specs=[
            SCALARS,
            seq_spec,
            same((win, width)),
            pl.BlockSpec((1, 1, win), lambda i: (i, 0, 0)),
            pl.BlockSpec((1, win, 1), lambda i: (i, 0, 0)),
            pl.BlockSpec((1, win, 3 * width), lambda i: (i, 0, 0)),
            pl.BlockSpec((1, H, win), lambda i: (i, 0, 0)),
            row_spec,
            row_spec,
            same(dnorm.shape),
        ]
        + [same(piece.shape) for piece in w]
        + [pl.BlockSpec(memory_space=pl.ANY) for _ in behind],
        out_specs=[seq_spec] + [whole(shape) for shape in grad_shapes],
        out_shape=[jax.ShapeDtypeStruct(x.shape, BF)]
        + [jax.ShapeDtypeStruct(shape, BF) for shape in grad_shapes],
        scratch_shapes=[
            pltpu.VMEM((win, win), F32),
            pltpu.VMEM((win, 3 * width), BF),
            pltpu.VMEM((tiles, width, tile), BF),
            pltpu.VMEM((tiles + width // tile + 1, width, tile), F32),
        ],
        compiler_params=memory(36),
        cost_estimate=takes(22),
        name="attend_backward",
    )(me, x, positions, ids[:, None, :], ids[:, :, None], qkv, lse, gmixed, mid, dnorm, *w, *behind)


def right_kernel(rows_ref, right_ref, out_ref):
    seqs, _, _ = out_ref.shape
    slots, _, tile = rows_ref.shape
    cols = tile // seqs
    for s in range(slots):
        turned = nn(rows_ref[s], right_ref[s]).astype(BF)
        for j in range(seqs):
            out_ref[j, :, s * cols : (s + 1) * cols] = turned[:, j * cols : (j + 1) * cols]


def right_turn(rows, right, seqs):
    slots, rows_dev, tile = rows.shape
    return pl.pallas_call(
        right_kernel,
        out_shape=jax.ShapeDtypeStruct((seqs, rows_dev, slots * tile // seqs), BF),
        compiler_params=PARAMS,
        cost_estimate=takes(3),
        name="right_turn",
    )(rows, right)


def left_kernel(x_ref, moments_ref, left_ref, left_t_ref, out_ref):
    seqs, rows_dev, wide = x_ref.shape
    slots, width, _ = left_ref.shape
    cols = wide // slots
    x = x_ref[...].reshape(width, wide)
    at = moments_ref.shape[2] - 2 * wide
    moments = moments_ref[:, :, at:].reshape(width, 2 * wide).astype(F32)
    turned = [nn(left_t_ref[s], x[:, s * cols : (s + 1) * cols]) for s in range(slots)]
    turned = jnp.concatenate(turned, axis=1)
    direction = adam_step(turned, moments[:, :wide], moments[:, wide:])[2].astype(BF)
    change = [nn(left_ref[s], direction[:, s * cols : (s + 1) * cols]) for s in range(slots)]
    out = jnp.concatenate(change + [turned], axis=1).astype(BF)
    out_ref[...] = out.reshape(out_ref.shape)


def left_turns(x, moments, left, left_t):
    seqs, rows_dev, wide = x.shape
    return pl.pallas_call(
        left_kernel,
        out_shape=jax.ShapeDtypeStruct((seqs, rows_dev, 2 * wide), BF),
        compiler_params=PARAMS,
        cost_estimate=takes(3),
        name="left_turns",
    )(x, moments, left, left_t)


def last_kernel(back_ref, right_ref, w_ref, one_ref, two_ref, new_one, new_two, new_w):
    seqs, rows_dev, _ = back_ref.shape
    slots, _, tile = w_ref.shape
    cols = tile // seqs
    for s in range(slots):

        def columns(first):
            return jnp.concatenate(
                [back_ref[j, :, first + s * cols : first + (s + 1) * cols] for j in range(seqs)], axis=1
            )

        change = nt(columns(0), right_ref[s])
        turned = columns(slots * cols).astype(F32)
        new_one[s], new_two[s], _ = adam_step(turned, one_ref[s], two_ref[s])
        old = w_ref[s]
        new_w[s] = old - LEARN * (change + DECAY * old)


def last_turn(back, right, weights, one, two):
    shape = jax.ShapeDtypeStruct(weights.shape, F32)
    return pl.pallas_call(
        last_kernel,
        out_shape=[shape, shape, shape],
        compiler_params=PARAMS,
        cost_estimate=takes(3),
        name="last_turn",
    )(back, right, weights, one, two)


def columns_kernel(one_ref, two_ref, out_ref):
    seqs = out_ref.shape[0]
    slots, _, tile = one_ref.shape
    cols = tile // seqs
    for first, ref in ((0, one_ref), (slots, two_ref)):
        for s in range(slots):
            values = ref[s].astype(BF)
            for j in range(seqs):
                at = (first + s) * cols
                out_ref[j, :, at : at + cols] = values[:, j * cols : (j + 1) * cols]


def moment_columns(one, two, seqs):
    slots, rows_dev, tile = one.shape
    return pl.pallas_call(
        columns_kernel,
        out_shape=jax.ShapeDtypeStruct((seqs, rows_dev, 2 * slots * tile // seqs), BF),
        compiler_params=PARAMS,
        cost_estimate=takes(3000),
        name="moment_columns",
    )(one, two)


def bases_kernel(left_ref, right_ref, low_left, low_left_t, low_right):
    left = left_ref[0].astype(BF)
    low_left[0] = left
    low_left_t[0] = left.T
    low_right[0] = right_ref[0].astype(BF)


def low_bases(left, right):
    slots, width, _ = left.shape
    tile = right.shape[1]
    big = pl.BlockSpec((1, width, width), lambda i: (i, 0, 0))
    little = pl.BlockSpec((1, tile, tile), lambda i: (i, 0, 0))
    return pl.pallas_call(
        bases_kernel,
        grid=(slots,),
        in_specs=[big, little],
        out_specs=[big, big, little],
        out_shape=[
            jax.ShapeDtypeStruct(left.shape, BF),
            jax.ShapeDtypeStruct(left.shape, BF),
            jax.ShapeDtypeStruct(right.shape, BF),
        ],
        compiler_params=PARAMS,
        cost_estimate=takes(3),
        name="low_bases",
    )(left, right)


def swap(x, axis, bit):
    size = lax.axis_size(axis)
    return lax.ppermute(x, axis, [(i, i ^ bit) for i in range(size)])


def exchange(x, axis, group):
    size = lax.axis_size(axis)
    groups = None
    if group != size:
        groups = [[base + i for i in range(group)] for base in range(0, size, group)]
    return lax.all_to_all(x, axis, 0, 0, axis_index_groups=groups, tiled=True)


def after(x, *others):
    return lax.optimization_barrier((x,) + others)[0]


def powers(first, size):
    bits = []
    while first < size:
        bits.append(first)
        first *= 2
    return bits


def gather(block, order):
    own = block[None]
    for axis, bit in order[:-1]:
        own = jnp.concatenate([own, swap(own, axis, bit)], axis=0)
    return own, swap(own, *order[-1])


def add(a, b, *others):
    if others:
        b = after(b, *others)
    return (a.astype(F32) + b.astype(F32)).astype(BF)


def double(buf, axis, bit, *others):
    got = swap(buf, axis, bit)
    if others:
        got = after(got, *others)
    return jnp.concatenate([buf, got], axis=0)


def halve(buf, axis, bit, *others):
    cut = buf.shape[0] // 2
    return add(buf[:cut], swap(buf[cut:], axis, bit), *others)


def body(
    inputs,
    cotangent,
    segments,
    owners,
    weights,
    left_bases,
    right_bases,
    moment_one,
    moment_two,
    norm_params,
    norm_one,
    norm_two,
    positions,
    pos_one,
    pos_two,
):
    seqs = lax.axis_size("seq")
    reps = lax.axis_size("rep")
    me_s = lax.axis_index("seq")
    me_r = lax.axis_index("rep")
    me = jnp.stack([me_s, me_r]).astype(jnp.int32)
    seq_local, span, width = inputs.shape
    rows_dev, slots, tile = weights.shape
    tiles = owners.shape[0]
    rows = rows_dev // reps
    group = WIN // span
    place = me_s % group
    wins = seq_local // group
    aligned = rows % 16 == 0
    blocks = seqs * reps
    seq_bits = [("seq", b) for b in powers(1, seqs)[::-1]]
    far_bits = [("rep", b) for b in powers(2, reps)]
    core_bit = [("rep", 1)]

    low_w = weights.astype(BF).transpose(1, 0, 2).reshape(slots, reps, rows, tile).transpose(1, 0, 2, 3)
    near = [lax.dynamic_index_in_dim(low_w, me_r, 0, keepdims=False)]
    for k in range(1, reps):
        near.append(swap(lax.dynamic_index_in_dim(low_w, me_r ^ k, 0, keepdims=False), "rep", k))
    near = jnp.concatenate(near, axis=0)
    near = jnp.take(near, ((owners // slots) ^ me_r) * slots + owners % slots, axis=0)
    ids = segments.reshape(-1)
    id_tiles = -(-2 * ids.shape[0] // (rows * tile))
    ids = jnp.concatenate([ids // 64, ids % 64]).astype(BF)
    ids = jnp.pad(ids, (0, id_tiles * rows * tile - ids.shape[0])).reshape(id_tiles, rows, tile)

    qkv_tiles = 3 * width // tile
    rest_tiles = tiles - qkv_tiles
    qkv_at, rest_at = qkv_tiles // 2, rest_tiles // 2
    split = qkv_at + id_tiles
    by_slot = [values.transpose(1, 0, 2) for values in (weights, moment_one, moment_two)]
    rest = near[qkv_tiles:][None]
    near = jnp.concatenate([near[:qkv_at], ids, near[qkv_at:qkv_tiles]], axis=0)[None]
    moments = moment_columns(after(by_slot[1], near), by_slot[2], seqs)
    for i, step in enumerate(seq_bits[:-1]):
        near = double(near, *step, *([moments] if i == 0 else []))
        rest = double(after(rest, moments) if i == 0 else rest, *step, near)
        if i == 0:
            x = after(inputs, near)
    x = exchange(x, "seq", group)
    cot = exchange(after(cotangent, x), "seq", group).reshape(group, wins, span, width)
    x = x.reshape(group, wins, span, width)

    def table_of(masks):
        table = np.zeros(blocks, np.int32)
        for k, (s, t) in enumerate(masks):
            table[s * reps + t] = k
        return jnp.asarray(table)

    orders = [seq_bits[-1:] + far_bits, far_bits + seq_bits[-1:]]

    def pieces_of(bufs, ranges):
        pieces, plans = [], []
        for buf, order, (first, last) in zip(bufs, orders, ranges):
            masks = gather_masks(seq_bits[:-1] + order)
            pieces += [buf, swap(buf, *core_bit[0])]
            plans += [(first, last, masks), (first, last, beyond(masks))]
        return settle(pieces, plans)

    def settle(pieces, plans):
        if aligned:
            return pieces, plans
        at = jnp.arange(blocks)
        full = []
        for i in range(0, len(pieces), 2):
            count = plans[i][1] - plans[i][0]
            table = table_of(plans[i][2] + plans[i + 1][2])
            both = jnp.concatenate([pieces[i][:, :count], pieces[i + 1][:, :count]], axis=0)
            both = jnp.take(both, table[((at // reps) ^ me_s) * reps + ((at % reps) ^ me_r)], axis=0)
            full.append(both.transpose(1, 0, 2, 3).reshape(count, blocks * rows, tile))
        return [jnp.concatenate(full, axis=0)], None

    bufs = [near[:, :split], near[:, split:]]
    bufs = [double(buf, *order[0]) for buf, order in zip(bufs, orders)]
    ids = bufs[0][:, qkv_at:]
    rest = after(rest, *bufs)
    for i in range(1, len(orders[0])):
        bufs = [double(buf, *order[i]) for buf, order in zip(bufs, orders)]
    w_qkv, qkv_plans = pieces_of(bufs, [(0, qkv_at), (qkv_at, qkv_tiles)])
    rest = [rest[:, :rest_at], rest[:, rest_at:]]
    rest = [double(buf, *order[0], *bufs) for buf, order in zip(rest, orders)]

    ids = ids.reshape(seqs, -1)[:, : 2 * seq_local * span].astype(jnp.int32)
    ids = (ids[:, : seq_local * span] * 64 + ids[:, seq_local * span :]).reshape(seqs, seq_local, span)
    spots = [0] * seqs
    for k, (s, _) in enumerate(gather_masks(seq_bits[:-1] + seq_bits[-1:])):
        spots[s] = k
    ids = jnp.take(ids, jnp.asarray(spots[:group])[jnp.arange(group) ^ place], axis=0)
    ids = lax.dynamic_slice_in_dim(ids, place * wins, wins, 1)
    ids = ids.transpose(1, 0, 2).reshape(wins, WIN)

    def scatter_plans(parts):
        count = parts[-1][1]
        if not aligned:
            return None, [(count, blocks * rows, tile)]
        own = [(first, last, gather_masks(order[:0:-1])) for first, last, order in parts]
        other = [(first, last, beyond(masks)) for first, last, masks in own]
        shape = (count * blocks // 2, rows, tile)
        return [own, other], [shape, shape]

    def scatter_tiles(grads, parts, *others):
        if not aligned:
            plain = grads[0].reshape(-1, blocks, rows, tile).transpose(1, 0, 2, 3)
            own, other = [], []
            for first, last, order in parts:
                masks = gather_masks(order[:0:-1])
                for target, some in ((own, masks), (other, beyond(masks))):
                    spots = np.array([s * reps + t for s, t in some])
                    at = ((spots // reps) ^ me_s) * reps + ((spots % reps) ^ me_r)
                    target.append(jnp.take(plain[:, first:last], at, axis=0).reshape(-1, rows, tile))
            grads = [jnp.concatenate(own, axis=0), jnp.concatenate(other, axis=0)]
        return add(grads[0], swap(grads[1], *core_bit[0]), *others)

    def cut_parts(buf, parts):
        out, at = [], 0
        for first, last, _ in parts:
            size = (last - first) * blocks // 2
            out.append(buf[at : at + size])
            at += size
        return out

    def join(bufs, parts):
        entries = 2 ** len(seq_bits[:-1])
        return jnp.concatenate([buf.reshape(entries, -1, rows, tile) for buf in bufs], axis=1)

    zyxc = seq_bits + far_bits + core_bit
    zxyc = seq_bits[:-1] + far_bits + seq_bits[-1:] + core_bit
    ids = after(ids, *rest)
    ahead = attend_forward(me, x, positions, ids, w_qkv, qkv_plans, qkv_tiles, tile, reps)
    for i in range(1, len(orders[0])):
        got = [swap(buf, *order[i]) for buf, order in zip(rest, orders)]
        qkv, mixed, lse, *got = lax.optimization_barrier((*ahead, *got))
        rest = [jnp.concatenate([buf, part], axis=0) for buf, part in zip(rest, got)]
    w_rest, rest_plans = pieces_of(rest, [(0, rest_at), (rest_at, rest_tiles)])
    rest_parts = [(0, rest_at, zyxc[::-1]), (rest_at, rest_tiles, zxyc[::-1])]
    out_plans, shapes = scatter_plans(rest_parts)
    result, mid, gmixed, d_norm, *d_rest = middle(
        me, x, positions, mixed, cot, norm_params, moments, group == seqs, w_rest, rest_plans, out_plans, shapes, rest_tiles, tile, reps, rows
    )
    result = exchange(result, "seq", group)
    rest = cut_parts(scatter_tiles(d_rest, rest_parts), rest_parts)
    steps = [[order[1 + i] for _, _, order in rest_parts] for i in range(len(orders[0]))]
    cuts = [buf.shape[0] // 2 for buf in rest]
    got = [swap(buf[cut:], *step) for buf, cut, step in zip(rest, cuts, steps[0])]

    qkv_total = qkv_tiles + width // tile + 1
    qkv_parts = [(0, 4, zyxc[::-1]), (4, qkv_total, zxyc[::-1])]
    out_plans, shapes = scatter_plans(qkv_parts)
    g_input, *d_qkv = attend_backward(
        me, x, positions, ids, qkv, lse, gmixed, mid, d_norm, rest,
        w_qkv, qkv_plans, out_plans, shapes, qkv_tiles, tile, reps, rows,
    )
    count = len(d_qkv)
    g_input, *some = lax.optimization_barrier((g_input, *d_qkv, *got))
    d_qkv, got = some[:count], some[count:]
    g_input = after(g_input, result)
    if group == seqs:
        moments = result
    else:
        moments = lax.all_to_all(after(moments, result), "seq", 0, 0, tiled=True)
    result = result[:, :, : wins * width].reshape(group, span, wins, width)
    result = result.transpose(0, 2, 1, 3).reshape(seq_local, span, width)
    rest = [add(buf[:cut], part) for buf, cut, part in zip(rest, cuts, got)]

    qkv_buf = scatter_tiles(d_qkv, qkv_parts)
    mine = cut_parts(qkv_buf, qkv_parts)
    low_left, low_left_t, low_right = low_bases(after(left_bases, qkv_buf), right_bases)
    mine = [halve(buf, *step, low_left) for buf, step in zip(mine, steps[0])]
    for some in steps[1:]:
        rest = [halve(buf, *step, *mine) for buf, step in zip(rest, some)]
        mine = [halve(buf, *step, *rest) for buf, step in zip(mine, some)]
    rest, mine = join(rest, rest_parts), join(mine, qkv_parts)
    for step in seq_bits[-2::-1]:
        rest = halve(rest, *step, mine)
        mine = halve(mine, *step, rest)
    rest, mine = rest[0], mine[0]
    g_input = exchange(g_input.reshape(seq_local, span, width), "seq", group)

    small = mine[qkv_tiles:]
    grad_norms = small[-1, : 4 * width // tile].astype(F32)
    sums = jnp.concatenate([mine[:qkv_tiles], rest], axis=0)
    tile_of = jnp.sum(
        jnp.where(owners[None, :] == jnp.arange(tiles)[:, None], jnp.arange(tiles)[None, :], 0), axis=1
    )
    sums = jnp.take(sums, tile_of, axis=0).reshape(reps, slots, rows, tile)
    small = small[: width // tile]
    near = []
    for k in range(reps):
        part = lax.dynamic_index_in_dim(sums, me_r ^ k, 0, keepdims=False)
        part = jnp.concatenate([part, small], axis=0)
        near.append(swap(part, "rep", k) if k else part)
    sums = jnp.take(jnp.stack(near), jnp.arange(reps) ^ me_r, axis=0)
    sums = sums.transpose(1, 0, 2, 3).reshape(-1, rows_dev, tile)
    small = sums[slots:]
    sums = sums[:slots]

    turned = right_turn(sums, low_right, seqs)
    small = after(small, turned)
    turned = lax.all_to_all(after(turned, g_input), "seq", 0, 0, tiled=True)
    back = left_turns(turned, moments, low_left, low_left_t)
    news = last_turn(lax.all_to_all(back, "seq", 0, 0, tiled=True), low_right, *by_slot)
    first_new, second_new, new_weights = [values.transpose(1, 0, 2) for values in news]

    own = small[None]
    for step in seq_bits:
        own = double(own, *step, back)
    masks = gather_masks(seq_bits)
    table = np.zeros(seqs, np.int32)
    for k, (i, _) in enumerate(masks):
        table[i] = k
    grad_pos = jnp.take(own, jnp.asarray(table)[jnp.arange(seqs) ^ me_s], axis=0)
    grad_pos = grad_pos.transpose(0, 2, 1, 3).reshape(WIN, width).astype(F32)
    if aligned:
        grad_norms = grad_norms.reshape(width // tile, 4, tile).transpose(1, 0, 2).reshape(4, width)
    else:
        grad_norms = lax.psum(d_norm, ("seq", "rep"))
    norm_first, norm_second, norm_dir = adam_step(grad_norms, norm_one, norm_two)
    pos_first, pos_second, pos_dir = adam_step(grad_pos, pos_one, pos_two)
    return (
        result,
        after(g_input, back).astype(F32),
        first_new,
        second_new,
        new_weights,
        norm_first,
        norm_second,
        norm_params - LEARN_SMALL * norm_dir,
        pos_first,
        pos_second,
        positions - LEARN_SMALL * pos_dir,
    )


def solution(mesh):
    tokens = P("rep", "seq", None)
    slots = P("seq", "rep", None)
    bases = P("rep", None, None)
    return jax.shard_map(
        body,
        mesh=mesh,
        in_specs=(
            tokens,
            tokens,
            P("rep", "seq"),
            P(),
            slots,
            bases,
            bases,
            slots,
            slots,
            P(),
            P(),
            P(),
            P(),
            P(),
            P(),
        ),
        out_specs=(tokens, tokens, slots, slots, slots, P(), P(), P(), P(), P(), P()),
        check_vma=False,
    )
```

profile of v0, /device:TPU:0, one launch (start us, length us, event | category | flops | bytes accessed | tf_op | source)
XLA Modules:
  0.0 266.7 jit_solution(17120559873327460146)
XLA Ops:
  16.5 5.3 %all-to-all-start = ((bf16[16,64,512]{2,1,0:T(8,128)(2,1)}), bf16[16,64,512]{2,1,0:T(8,128)(2,1)S(1)}, u32[]{:S(2)}, u32[]{:S(2)}) async-start(bf16[16,64,512]{2,1,0:T(8,128)(2,1)} %param.19), calls=%async_computation | async-start | bytes 2097152 | tf_op jit(solution)/shard_map/all_to_all | solution.py:629
  30.7 5.2 %collective-permute-done.5 = bf16[4,4,16,256]{3,2,1,0:T(8,128)(2,1)S(1)} collective-permute-done((bf16[4,4,16,256]{3,2,1,0:T(8,128)(2,1)S(1)}, bf16[4,4,16,256]{3,2,1,0:T(8,128)(2,1)S(1)}, u32[]{:S(2)}, u32[]{:S(2)}) %collective-permute-start.5) | collective-permute-done | bytes 131104 | tf_op jit(solution)/shard_map/ppermute | solution.py:621
  37.1 7.9 %collective-permute-done.7 = bf16[2,18,16,256]{3,2,1,0:T(8,128)(2,1)S(1)} collective-permute-done((bf16[2,18,16,256]{3,2,1,0:T(8,128)(2,1)S(1)}, bf16[2,18,16,256]{3,2,1,0:T(8,128)(2,1)S(1)}, u32[]{:S(2)}, u32[]{:S(2)}) %collective-permute-start.7) | collective-permute-done | bytes 294944 | tf_op jit(solution)/shard_map/ppermute | solution.py:621
  48.7 4.1 %collective-permute-done.12 = bf16[4,9,16,256]{3,2,1,0:T(8,128)(2,1)S(1)} collective-permute-done((bf16[4,9,16,256]{3,2,1,0:T(8,128)(2,1)S(1)}, bf16[4,9,16,256]{3,2,1,0:T(8,128)(2,1)S(1)}, u32[]{:S(2)}, u32[]{:S(2)}) %collective-permute-start.12) | collective-permute-done | bytes 294944 | tf_op jit(solution)/shard_map/ppermute | solution.py:621
  58.6 6.8 %all-to-all-start.1 = ((bf16[16,64,512]{2,1,0:T(8,128)(2,1)}), bf16[16,64,512]{2,1,0:T(8,128)(2,1)}, u32[]{:S(2)}, u32[]{:S(2)}) async-start(bf16[16,64,512]{2,1,0:T(8,128)(2,1)} %param.20), calls=%async_computation.1 | async-start | bytes 2097152 | tf_op jit(solution)/shard_map/all_to_all | solution.py:629
  66.5 7.5 %attend_forward.1 = (bf16[2,512,1536]{2,1,0:T(8,128)(2,1)S(1)}, bf16[2,512,512]{2,1,0:T(8,128)(2,1)S(1)}, f32[2,8,512]{2,1,0:T(8,128)S(1)}) custom-call(s32[2]{0:T(128)S(1)} %pad_add_fusion.me_ref, bf16[8,2,64,512]{3,2,1,0:T(8,128)(2,1)S(1)} %bitcast.86, f32[512,512]{1,0:T(8,128)S(1)} %copy-done, s32[2,1,512]{2,1,0:T(1,128)S(1)} %broadcast_in_dim.77.ids_row, ...), custom_call_target="tpu_custom_call" | custom-call | flops 18000000 | tf_op jit(solution)/shard_map/attend_forward/pallas_call | solution.py:184
  82.0 9.7 %all-to-all-done.1 = bf16[16,64,512]{2,1,0:T(8,128)(2,1)} async-done(((bf16[16,64,512]{2,1,0:T(8,128)(2,1)}), bf16[16,64,512]{2,1,0:T(8,128)(2,1)}, u32[]{:S(2)}, u32[]{:S(2)}) %all-to-all-start.1) | async-done | bytes 1048608 | tf_op jit(solution)/shard_map/all_to_all | solution.py:629
  91.8 29.0 %middle.1 = (bf16[8,64,1408]{2,1,0:T(8,128)(2,1)}, f32[2,512,512]{2,1,0:T(8,128)}, bf16[2,512,512]{2,1,0:T(8,128)(2,1)}, f32[4,512]{1,0:T(4,128)}, bf16[288,16,2...) custom-call(s32[2]{0:T(128)} %copy-done.12, bf16[8,2,64,512]{3,2,1,0:T(8,128)(2,1)} %bitcast.87, f32[512,512]{1,0:T(8,128)} %pos_ref.5, ...), custom_call_target="tpu_custom_call" | custom-call | flops 27000000 | tf_op jit(solution)/shard_map/middle/pallas_call | solution.py:309
  120.8 4.5 %all-to-all-start.2 = ((bf16[8,64,1408]{2,1,0:T(8,128)(2,1)}), bf16[8,64,1408]{2,1,0:T(8,128)(2,1)}, u32[]{:S(2)}, u32[]{:S(2)}) async-start(bf16[8,64,1408]{2,1,0:T(8,128)(2,1)} %get-tuple-element.86), calls=%async_computation.2 | async-start | bytes 2883584 | tf_op jit(solution)/shard_map/all_to_all | solution.py:629
  125.7 3.2 %add_convert_fusion = bf16[288,16,256]{2,1,0:T(8,128)(2,1)S(1)} fusion(bf16[288,16,256]{2,1,0:T(8,128)(2,1)} %collective-permute-done.19, bf16[288,16,256]{2,1,0:T(8,128)(2,1)} %get-tuple-element.92), kind=kLoop, calls=%fused_computation.7 | loop fusion | flops 4718592 | bytes 7077888 | tf_op jit(solution)/shard_map/convert_element_type | solution.py:654
  132.3 14.8 %attend_backward.1 = (bf16[8,2,64,512]{3,2,1,0:T(8,128)(2,1)}, bf16[144,16,256]{2,1,0:T(8,128)(2,1)S(1)}, bf16[144,16,256]{2,1,0:T(8,128)(2,1)S(1)}) custom-call(s32[2]{0:T(128)S(1)} %copy-done.13, bf16[8,2,64,512]{3,2,1,0:T(8,128)(2,1)S(1)} %bitcast.88, f32[512,512]{1,0:T(8,128)S(1)} %copy-done.1, s32[2,1,512]{2,1,0:T(1,128)S(1)} %broadcast_in_dim.77.ids_row, ...), custom_call_target="tpu_custom_call" | custom-call | flops 22000000 | tf_op jit(solution)/shard_map/attend_backward/pallas_call | solution.py:460
  147.1 9.3 %collective-permute-done.21 = bf16[72,16,256]{2,1,0:T(8,128)(2,1)S(1)} collective-permute-done((bf16[72,16,256]{2,1,0:T(8,128)(2,1)S(1)}, bf16[72,16,256]{2,1,0:T(8,128)(2,1)S(1)}, u32[]{:S(2)}, u32[]{:S(2)}) %collective-permute-start.21) | collective-permute-done | bytes 589856 | tf_op jit(solution)/shard_map/ppermute | solution.py:621
  167.0 4.9 %all-to-all-start.3 = ((bf16[16,64,512]{2,1,0:T(8,128)(2,1)}), bf16[16,64,512]{2,1,0:T(8,128)(2,1)S(1)}, u32[]{:S(2)}, u32[]{:S(2)}) async-start(bf16[16,64,512]{2,1,0:T(8,128)(2,1)} %bitcast.21), calls=%async_computation.3 | async-start | bytes 2097152 | tf_op jit(solution)/shard_map/all_to_all | solution.py:629
  172.0 7.3 %low_bases.1 = (bf16[6,512,512]{2,1,0:T(8,128)(2,1)}, bf16[6,512,512]{2,1,0:T(8,128)(2,1)}, bf16[6,256,256]{2,1,0:T(8,128)(2,1)}) custom-call(f32[6,512,512]{2,1,0:T(8,128)} %left_ref, f32[6,256,256]{2,1,0:T(8,128)} %right_ref.1), custom_call_target="tpu_custom_call" | custom-call | flops 3000000 | tf_op jit(solution)/shard_map/low_bases/pallas_call | solution.py:603
  187.2 4.9 %collective-permute-done.24 = bf16[16,16,256]{2,1,0:T(8,128)(2,1)S(1)} collective-permute-done((bf16[16,16,256]{2,1,0:T(8,128)(2,1)S(1)}, bf16[16,16,256]{2,1,0:T(8,128)(2,1)S(1)}, u32[]{:S(2)}, u32[]{:S(2)}) %collective-permute-start.24) | collective-permute-done | bytes 131104 | tf_op jit(solution)/shard_map/ppermute | solution.py:621
  193.8 6.5 %collective-permute-done.30 = bf16[2,18,16,256]{3,2,1,0:T(8,128)(2,1)S(1)} collective-permute-done((bf16[2,18,16,256]{3,2,1,0:T(8,128)(2,1)S(1)}, bf16[2,18,16,256]{3,2,1,0:T(8,128)(2,1)S(1)}, u32[]{:S(2)}, u32[]{:S(2)}) %collective-permute-start.30) | collective-permute-done | bytes 294944 | tf_op jit(solution)/shard_map/ppermute | solution.py:621
  204.2 4.6 %collective-permute-done.32 = bf16[1,18,16,256]{3,2,1,0:T(8,128)(2,1)S(1)} collective-permute-done((bf16[1,18,16,256]{3,2,1,0:T(8,128)(2,1)S(1)}, bf16[1,18,16,256]{3,2,1,0:T(8,128)(2,1)S(1)}, u32[]{:S(2)}, u32[]{:S(2)}) %collective-permute-start.32) | collective-permute-done | bytes 147488 | tf_op jit(solution)/shard_map/ppermute | solution.py:621
  213.1 3.1 %collective-permute-done.34 = bf16[8,16,256]{2,1,0:T(8,128)(2,1)S(1)} collective-permute-done((bf16[8,16,256]{2,1,0:T(8,128)(2,1)S(1)}, bf16[8,16,256]{2,1,0:T(8,128)(2,1)S(1)}, u32[]{:S(2)}, u32[]{:S(2)}) %collective-permute-start.34) | collective-permute-done | bytes 65568 | tf_op jit(solution)/shard_map/ppermute | solution.py:621
  220.6 3.9 %all-to-all-start.4 = ((bf16[8,64,192]{2,1,0:T(8,128)(2,1)}), bf16[8,64,192]{2,1,0:T(8,128)(2,1)S(1)}, u32[]{:S(2)}, u32[]{:S(2)}) async-start(bf16[8,64,192]{2,1,0:T(8,128)(2,1)} %right_turn.1), calls=%async_computation.4 | async-start | bytes 524288 | tf_op jit(solution)/shard_map/all_to_all | solution.py:887
  229.8 6.0 %all-to-all-done.4.x_ref = bf16[8,64,192]{2,1,0:T(8,128)(2,1)S(1)} async-done(((bf16[8,64,192]{2,1,0:T(8,128)(2,1)}), bf16[8,64,192]{2,1,0:T(8,128)(2,1)S(1)}, u32[]{:S(2)}, u32[]{:S(2)}) %all-to-all-start.4) | async-done | bytes 196640 | tf_op jit(solution)/shard_map/all_to_all | solution.py:887
  236.5 6.5 %left_turns.1 = bf16[8,64,384]{2,1,0:T(8,128)(2,1)} custom-call(bf16[8,64,192]{2,1,0:T(8,128)(2,1)} %copy-done.33, bf16[8,64,1408]{2,1,0:T(8,128)(2,1)} %all-to-all-done.2.moments_ref, bf16[6,512,512]{2,1,0:T(8,128)(2,1)} %get-tuple-element.102.left_ref, bf16[6,512,512]{2,1,0:T(8,128)(2,1)} %get-tuple-element.117.left_t_ref), custom_call_target="tpu_custom_call" | custom-call | flops 3000000 | tf_op jit(solution)/shard_map/left_turns/pallas_call | solution.py:530
  244.2 3.9 %collective-permute-done.37 = bf16[2,2,64,256]{3,2,1,0:T(8,128)(2,1)S(1)} collective-permute-done((bf16[2,2,64,256]{3,2,1,0:T(8,128)(2,1)S(1)}, bf16[2,2,64,256]{3,2,1,0:T(8,128)(2,1)S(1)}, u32[]{:S(2)}, u32[]{:S(2)}) %collective-permute-start.37) | collective-permute-done | bytes 131104 | tf_op jit(solution)/shard_map/ppermute | solution.py:621
  250.3 3.5 %all-to-all-start.5 = ((bf16[8,64,384]{2,1,0:T(8,128)(2,1)}), bf16[8,64,384]{2,1,0:T(8,128)(2,1)S(1)}, u32[]{:S(2)}, u32[]{:S(2)}) async-start(bf16[8,64,384]{2,1,0:T(8,128)(2,1)} %left_turns.1), calls=%async_computation.5 | async-start | bytes 786432 | tf_op jit(solution)/shard_map/all_to_all | solution.py:889
  263.7 3.0 %last_turn.1 = (f32[6,64,256]{2,1,0:T(8,128)}, f32[6,64,256]{2,1,0:T(8,128)}, f32[6,64,256]{2,1,0:T(8,128)}) custom-call(bf16[8,64,384]{2,1,0:T(8,128)(2,1)} %copy-done.25, bf16[6,256,256]{2,1,0:T(8,128)(2,1)} %get-tuple-element.115.right_ref, f32[6,64,256]{2,1,0:T(8,128)} %bitcast.95, f32[6,64,256]{2,1,0:T(8,128)} %bitcast.110, f32[6,64,256]{2,1,0:T(8,128)} %bitcast.112), custom_call_target="tpu_custom_call" | custom-call | flops 3000000 | tf_op jit(solution)/shard_map/last_turn/pallas_call | solution.py:559
  (272 shorter events, 99.6 us)
Async XLA Ops:
  14.5 9.8 %collective-permute-start.6 = (bf16[1,18,16,256]{3,2,1,0:T(8,128)(2,1)S(1)}, bf16[1,18,16,256]{3,2,1,0:T(8,128)(2,1)S(1)}, u32[]{:S(2)}, u32[]{:S(2)}) collective-permute-start(bf16[1,18,16,256]{3,2,1,0:T(8,128)(2,1)S(1)} %slice_bitcast_fusion), channel_id=1, source_target_pairs={{0,16},{4,20},{8,24},{12,28},{16,0},{20,4},{24,8},{28,12},{1,17},{... | collective-permute-start | bytes 442376 | tf_op jit(solution)/shard_map/ppermute | solution.py:621
  16.5 42.1 %all-to-all-start = ((bf16[16,64,512]{2,1,0:T(8,128)(2,1)}), bf16[16,64,512]{2,1,0:T(8,128)(2,1)S(1)}, u32[]{:S(2)}, u32[]{:S(2)}) async-start(bf16[16,64,512]{2,1,0:T(8,128)(2,1)} %param.19), calls=%async_computation | async-start | bytes 2097152 | tf_op jit(solution)/shard_map/all_to_all | solution.py:629
  24.3 20.7 %collective-permute-start.7 = (bf16[2,18,16,256]{3,2,1,0:T(8,128)(2,1)S(1)}, bf16[2,18,16,256]{3,2,1,0:T(8,128)(2,1)S(1)}, u32[]{:S(2)}, u32[]{:S(2)}) collective-permute-start(bf16[2,18,16,256]{3,2,1,0:T(8,128)(2,1)S(1)} %pad_maximum_fusion.12), channel_id=1, source_target_pairs={{0,8},{4,12},{8,0},{12,4},{16,24},{20,28},{24,16},{28,20},{1,9},{5... | collective-permute-start | bytes 884744 | tf_op jit(solution)/shard_map/ppermute | solution.py:621
  25.6 10.3 %collective-permute-start.5 = (bf16[4,4,16,256]{3,2,1,0:T(8,128)(2,1)S(1)}, bf16[4,4,16,256]{3,2,1,0:T(8,128)(2,1)S(1)}, u32[]{:S(2)}, u32[]{:S(2)}) collective-permute-start(bf16[4,4,16,256]{3,2,1,0:T(8,128)(2,1)S(1)} %slice.230), channel_id=1, source_target_pairs={{0,4},{4,0},{8,12},{12,8},{16,20},{20,16},{24,28},{28,24},{1,5},{5... | collective-permute-start | bytes 393224 | tf_op jit(solution)/shard_map/ppermute | solution.py:621
  29.2 19.4 %collective-permute-start.11 = (bf16[8,3,16,256]{3,2,1,0:T(8,128)(2,1)S(1)}, bf16[8,3,16,256]{3,2,1,0:T(8,128)(2,1)S(1)}, u32[]{:S(2)}, u32[]{:S(2)}) collective-permute-start(bf16[8,3,16,256]{3,2,1,0:T(8,128)(2,1)S(1)} %pad_maximum_fusion.17), channel_id=1, source_target_pairs={{0,4},{4,0},{8,12},{12,8},{16,20},{20,16},{24,28},{28,24},{1,5},{5... | collective-permute-start | bytes 589832 | tf_op jit(solution)/shard_map/ppermute | solution.py:621
  36.0 12.6 %collective-permute-start.10 = (bf16[8,4,16,256]{3,2,1,0:T(8,128)(2,1)S(1)}, bf16[8,4,16,256]{3,2,1,0:T(8,128)(2,1)S(1)}, u32[]{:S(2)}, u32[]{:S(2)}) collective-permute-start(bf16[8,4,16,256]{3,2,1,0:T(8,128)(2,1)S(1)} %pad_maximum_fusion.10), channel_id=1, source_target_pairs={{0,2},{1,3},{2,0},{3,1},{4,6},{5,7},{6,4},{7,5},{8,10},{9,11},{10,... | collective-permute-start | bytes 786440 | tf_op jit(solution)/shard_map/ppermute | solution.py:621
  48.6 17.8 %collective-permute-start.13 = (bf16[16,4,16,256]{3,2,1,0:T(8,128)(2,1)S(1)}, bf16[16,4,16,256]{3,2,1,0:T(8,128)(2,1)}, u32[]{:S(2)}, u32[]{:S(2)}) collective-permute-start(bf16[16,4,16,256]{3,2,1,0:T(8,128)(2,1)S(1)} %pad_maximum_fusion.6.refs_0_), channel_id=1, source_target_pairs={{0,1},{1,0},{2,3},{3,2},{4,5},{5,4},{6,7},{7,6},{8,9},{9,8},{10,11... | collective-permute-start | bytes 1572872 | tf_op jit(solution)/shard_map/ppermute | solution.py:621
  54.8 20.9 %collective-permute-start.16 = (bf16[8,9,16,256]{3,2,1,0:T(8,128)(2,1)}, bf16[8,9,16,256]{3,2,1,0:T(8,128)(2,1)}, u32[]{:S(2)}, u32[]{:S(2)}) collective-permute-start(bf16[8,9,16,256]{3,2,1,0:T(8,128)(2,1)} %pad_maximum_fusion.5), channel_id=1, source_target_pairs={{0,4},{4,0},{8,12},{12,8},{16,20},{20,16},{24,28},{28,24},{1,5},{5... | collective-permute-start | bytes 1769480 | tf_op jit(solution)/shard_map/ppermute | solution.py:621
  57.4 18.3 %collective-permute-start.15 = (bf16[8,9,16,256]{3,2,1,0:T(8,128)(2,1)}, bf16[8,9,16,256]{3,2,1,0:T(8,128)(2,1)}, u32[]{:S(2)}, u32[]{:S(2)}) collective-permute-start(bf16[8,9,16,256]{3,2,1,0:T(8,128)(2,1)} %pad_maximum_fusion.4), channel_id=1, source_target_pairs={{0,2},{1,3},{2,0},{3,1},{4,6},{5,7},{6,4},{7,5},{8,10},{9,11},{10,... | collective-permute-start | bytes 1769480 | tf_op jit(solution)/shard_map/ppermute | solution.py:621
  58.6 33.1 %all-to-all-start.1 = ((bf16[16,64,512]{2,1,0:T(8,128)(2,1)}), bf16[16,64,512]{2,1,0:T(8,128)(2,1)}, u32[]{:S(2)}, u32[]{:S(2)}) async-start(bf16[16,64,512]{2,1,0:T(8,128)(2,1)} %param.20), calls=%async_computation.1 | async-start | bytes 2097152 | tf_op jit(solution)/shard_map/all_to_all | solution.py:629
  120.8 46.2 %all-to-all-start.2 = ((bf16[8,64,1408]{2,1,0:T(8,128)(2,1)}), bf16[8,64,1408]{2,1,0:T(8,128)(2,1)}, u32[]{:S(2)}, u32[]{:S(2)}) async-start(bf16[8,64,1408]{2,1,0:T(8,128)(2,1)} %get-tuple-element.86), calls=%async_computation.2 | async-start | bytes 2883584 | tf_op jit(solution)/shard_map/all_to_all | solution.py:629
  129.0 18.1 %collective-permute-start.20 = (bf16[72,16,256]{2,1,0:T(8,128)(2,1)S(1)}, bf16[72,16,256]{2,1,0:T(8,128)(2,1)S(1)}, u32[]{:S(2)}, u32[]{:S(2)}) collective-permute-start(bf16[72,16,256]{2,1,0:T(8,128)(2,1)S(1)} %get-tuple-element.137), channel_id=1, source_target_pairs={{0,2},{1,3},{2,0},{3,1},{4,6},{5,7},{6,4},{7,5},{8,10},{9,11},{10,... | collective-permute-start | bytes 1769480 | tf_op jit(solution)/shard_map/ppermute | solution.py:621
  130.4 26.0 %collective-permute-start.21 = (bf16[72,16,256]{2,1,0:T(8,128)(2,1)S(1)}, bf16[72,16,256]{2,1,0:T(8,128)(2,1)S(1)}, u32[]{:S(2)}, u32[]{:S(2)}) collective-permute-start(bf16[72,16,256]{2,1,0:T(8,128)(2,1)S(1)} %get-tuple-element.136), channel_id=1, source_target_pairs={{0,4},{4,0},{8,12},{12,8},{16,20},{20,16},{24,28},{28,24},{1,5},{5... | collective-permute-start | bytes 1769480 | tf_op jit(solution)/shard_map/ppermute | solution.py:621
  161.0 18.2 %collective-permute-start.23 = (bf16[32,16,256]{2,1,0:T(8,128)(2,1)}, bf16[32,16,256]{2,1,0:T(8,128)(2,1)S(1)}, u32[]{:S(2)}, u32[]{:S(2)}) collective-permute-start(bf16[32,16,256]{2,1,0:T(8,128)(2,1)} %slice.245), channel_id=1, source_target_pairs={{0,2},{1,3},{2,0},{3,1},{4,6},{5,7},{6,4},{7,5},{8,10},{9,11},{10,... | collective-permute-start | bytes 786440 | tf_op jit(solution)/shard_map/ppermute | solution.py:621
  162.3 19.1 %collective-permute-start.26 = (bf16[40,16,256]{2,1,0:T(8,128)(2,1)}, bf16[40,16,256]{2,1,0:T(8,128)(2,1)}, u32[]{:S(2)}, u32[]{:S(2)}) collective-permute-start(bf16[40,16,256]{2,1,0:T(8,128)(2,1)} %slice.252), channel_id=1, source_target_pairs={{0,4},{4,0},{8,12},{12,8},{16,20},{20,16},{24,28},{28,24},{1,5},{5... | collective-permute-start | bytes 983048 | tf_op jit(solution)/shard_map/ppermute | solution.py:621
  163.5 19.0 %collective-permute-start.27 = (bf16[36,16,256]{2,1,0:T(8,128)(2,1)}, bf16[36,16,256]{2,1,0:T(8,128)(2,1)}, u32[]{:S(2)}, u32[]{:S(2)}) collective-permute-start(bf16[36,16,256]{2,1,0:T(8,128)(2,1)} %slice.255), channel_id=1, source_target_pairs={{0,2},{1,3},{2,0},{3,1},{4,6},{5,7},{6,4},{7,5},{8,10},{9,11},{10,... | collective-permute-start | bytes 884744 | tf_op jit(solution)/shard_map/ppermute | solution.py:621
  165.0 20.2 %collective-permute-start.25 = (bf16[36,16,256]{2,1,0:T(8,128)(2,1)}, bf16[36,16,256]{2,1,0:T(8,128)(2,1)}, u32[]{:S(2)}, u32[]{:S(2)}) collective-permute-start(bf16[36,16,256]{2,1,0:T(8,128)(2,1)} %slice.250), channel_id=1, source_target_pairs={{0,4},{4,0},{8,12},{12,8},{16,20},{20,16},{24,28},{28,24},{1,5},{5... | collective-permute-start | bytes 884744 | tf_op jit(solution)/shard_map/ppermute | solution.py:621
  167.0 53.6 %all-to-all-start.3 = ((bf16[16,64,512]{2,1,0:T(8,128)(2,1)}), bf16[16,64,512]{2,1,0:T(8,128)(2,1)S(1)}, u32[]{:S(2)}, u32[]{:S(2)}) async-start(bf16[16,64,512]{2,1,0:T(8,128)(2,1)} %bitcast.21), calls=%async_computation.3 | async-start | bytes 2097152 | tf_op jit(solution)/shard_map/all_to_all | solution.py:629
  179.4 12.8 %collective-permute-start.24 = (bf16[16,16,256]{2,1,0:T(8,128)(2,1)S(1)}, bf16[16,16,256]{2,1,0:T(8,128)(2,1)S(1)}, u32[]{:S(2)}, u32[]{:S(2)}) collective-permute-start(bf16[16,16,256]{2,1,0:T(8,128)(2,1)S(1)} %slice.247), channel_id=1, source_target_pairs={{0,4},{4,0},{8,12},{12,8},{16,20},{20,16},{24,28},{28,24},{1,5},{5... | collective-permute-start | bytes 393224 | tf_op jit(solution)/shard_map/ppermute | solution.py:621
  186.3 14.1 %collective-permute-start.30 = (bf16[2,18,16,256]{3,2,1,0:T(8,128)(2,1)S(1)}, bf16[2,18,16,256]{3,2,1,0:T(8,128)(2,1)S(1)}, u32[]{:S(2)}, u32[]{:S(2)}) collective-permute-start(bf16[2,18,16,256]{3,2,1,0:T(8,128)(2,1)S(1)} %pad_maximum_fusion.11), channel_id=1, source_target_pairs={{0,8},{4,12},{8,0},{12,4},{16,24},{20,28},{24,16},{28,20},{1,9},{5... | collective-permute-start | bytes 884744 | tf_op jit(solution)/shard_map/ppermute | solution.py:621
  192.2 10.4 %collective-permute-start.29 = (bf16[2,9,16,256]{3,2,1,0:T(8,128)(2,1)S(1)}, bf16[2,9,16,256]{3,2,1,0:T(8,128)(2,1)S(1)}, u32[]{:S(2)}, u32[]{:S(2)}) collective-permute-start(bf16[2,9,16,256]{3,2,1,0:T(8,128)(2,1)S(1)} %fusion.3), channel_id=1, source_target_pairs={{0,8},{4,12},{8,0},{12,4},{16,24},{20,28},{24,16},{28,20},{1,9},{5... | collective-permute-start | bytes 442376 | tf_op jit(solution)/shard_map/ppermute | solution.py:621
  220.6 15.2 %all-to-all-start.4 = ((bf16[8,64,192]{2,1,0:T(8,128)(2,1)}), bf16[8,64,192]{2,1,0:T(8,128)(2,1)S(1)}, u32[]{:S(2)}, u32[]{:S(2)}) async-start(bf16[8,64,192]{2,1,0:T(8,128)(2,1)} %right_turn.1), calls=%async_computation.4 | async-start | bytes 524288 | tf_op jit(solution)/shard_map/all_to_all | solution.py:887
  225.8 17.3 %collective-permute-start.36 = (bf16[1,2,64,256]{3,2,1,0:T(8,128)(2,1)S(1)}, bf16[1,2,64,256]{3,2,1,0:T(8,128)(2,1)S(1)}, u32[]{:S(2)}, u32[]{:S(2)}) collective-permute-start(bf16[1,2,64,256]{3,2,1,0:T(8,128)(2,1)S(1)} %bitcast.101), channel_id=1, source_target_pairs={{0,16},{4,20},{8,24},{12,28},{16,0},{20,4},{24,8},{28,12},{1,17},{... | collective-permute-start | bytes 196616 | tf_op jit(solution)/shard_map/ppermute | solution.py:621
  250.3 12.6 %all-to-all-start.5 = ((bf16[8,64,384]{2,1,0:T(8,128)(2,1)}), bf16[8,64,384]{2,1,0:T(8,128)(2,1)S(1)}, u32[]{:S(2)}, u32[]{:S(2)}) async-start(bf16[8,64,384]{2,1,0:T(8,128)(2,1)} %left_turns.1), calls=%async_computation.5 | async-start | bytes 786432 | tf_op jit(solution)/shard_map/all_to_all | solution.py:889
  (64 other events, 393.6 us)
where the time goes:
time: 268 us; the launch traced here: 267 us
  waiting for transfers between devices  82.7 us (31%)
  Pallas kernels  73 us (27%)
  starting transfers between devices  70.7 us (26%)
  other arithmetic  21.6 us (8%)
  local copies, waits for them, and re-layouts  16.9 us (6%)
    ppermute x39, waiting for transfers between devices, swap(): return lax.ppermute(x, axis, [(i, i ^ bit) for i in range(size)])  65.5 us
    ppermute x39, starting transfers between devices, swap(): return lax.ppermute(x, axis, [(i, i ^ bit) for i in range(size)])  41.8 us
    pallas_call x1, Pallas kernels, middle(): pl.pallas_call(functools.partial(middle_kernel, plans, out_plans, reps, r...  29 us
    all_to_all x4, starting transfers between devices, exchange(): return lax.all_to_all(x, axis, 0, 0, axis_index_groups=groups, tiled=True)  21.6 us
    pallas_call x1, Pallas kernels, attend_backward(): pl.pallas_call(functools.partial(attend_back_kernel, plans, out_plans, re...  14.8 us
    all_to_all x4, waiting for transfers between devices, exchange(): return lax.all_to_all(x, axis, 0, 0, axis_index_groups=groups, tiled=True)  9.73 us
    pallas_call x1, Pallas kernels, attend_forward(): pl.pallas_call(functools.partial(attend_kernel, plans, reps), grid=(wins,...  7.46 us
    convert_element_type x13, other arithmetic, add(): return (a.astype(F32) + b.astype(F32)).astype(BF)  7.4 us
  transfers between devices with their start and end apart: 45, of which 25 were waited for; matrix products, arithmetic and copies ran while one was open for 12% of the time, Pallas kernels for 15%

commit v1 on v0

--- a/solution.py
+++ b/solution.py
@@ -504,28 +504,30 @@
     return pl.pallas_call(
         right_kernel,
         out_shape=jax.ShapeDtypeStruct((seqs, rows_dev, slots * tile // seqs), BF),
-        compiler_params=PARAMS,
+        compiler_params=memory(16),
         cost_estimate=takes(3),
         name="right_turn",
     )(rows, right)
 
 
-def left_kernel(x_ref, moments_ref, left_ref, left_t_ref, out_ref):
+def left_kernel(x_ref, moments_ref, left_ref, out_ref):
     seqs, rows_dev, wide = x_ref.shape
     slots, width, _ = left_ref.shape
     cols = wide // slots
     x = x_ref[...].reshape(width, wide)
     at = moments_ref.shape[2] - 2 * wide
     moments = moments_ref[:, :, at:].reshape(width, 2 * wide).astype(F32)
-    turned = [nn(left_t_ref[s], x[:, s * cols : (s + 1) * cols]) for s in range(slots)]
-    turned = jnp.concatenate(turned, axis=1)
+    spare = -wide % 128
+    x_t = jnp.concatenate([x, jnp.zeros((width, spare), BF)], axis=1).T
+    turned = [nn(x_t[s * cols : (s + 1) * cols], left_ref[s]) for s in range(slots)]
+    turned = jnp.concatenate(turned + [jnp.zeros((spare, width), F32)], axis=0).T[:, :wide]
     direction = adam_step(turned, moments[:, :wide], moments[:, wide:])[2].astype(BF)
     change = [nn(left_ref[s], direction[:, s * cols : (s + 1) * cols]) for s in range(slots)]
     out = jnp.concatenate(change + [turned], axis=1).astype(BF)
     out_ref[...] = out.reshape(out_ref.shape)
 
 
-def left_turns(x, moments, left, left_t):
+def left_turns(x, moments, left):
     seqs, rows_dev, wide = x.shape
     return pl.pallas_call(
         left_kernel,
@@ -533,7 +535,7 @@
         compiler_params=PARAMS,
         cost_estimate=takes(3),
         name="left_turns",
-    )(x, moments, left, left_t)
+    )(x, moments, left)
 
 
 def last_kernel(back_ref, right_ref, w_ref, one_ref, two_ref, new_one, new_two, new_w):
@@ -559,7 +561,7 @@
     return pl.pallas_call(
         last_kernel,
         out_shape=[shape, shape, shape],
-        compiler_params=PARAMS,
+        compiler_params=memory(16),
         cost_estimate=takes(3),
         name="last_turn",
     )(back, right, weights, one, two)
@@ -588,25 +590,23 @@
     )(one, two)
 
 
-def bases_kernel(left_ref, right_ref, low_left, low_left_t, low_right):
-    left = left_ref[0].astype(BF)
-    low_left[0] = left
-    low_left_t[0] = left.T
-    low_right[0] = right_ref[0].astype(BF)
+def bases_kernel(left_ref, right_ref, low_left, low_right):
+    low_left[...] = left_ref[...].astype(BF)
+    low_right[...] = right_ref[...].astype(BF)
 
 
 def low_bases(left, right):
     slots, width, _ = left.shape
     tile = right.shape[1]
-    big = pl.BlockSpec((1, width, width), lambda i: (i, 0, 0))
-    little = pl.BlockSpec((1, tile, tile), lambda i: (i, 0, 0))
+    some = 3 if slots % 3 == 0 else 1
+    big = pl.BlockSpec((some, width, width), lambda i: (i, 0, 0))
+    little = pl.BlockSpec((some, tile, tile), lambda i: (i, 0, 0))
     return pl.pallas_call(
         bases_kernel,
-        grid=(slots,),
+        grid=(slots // some,),
         in_specs=[big, little],
-        out_specs=[big, big, little],
+        out_specs=[big, little],
         out_shape=[
-            jax.ShapeDtypeStruct(left.shape, BF),
             jax.ShapeDtypeStruct(left.shape, BF),
             jax.ShapeDtypeStruct(right.shape, BF),
         ],
@@ -832,7 +832,7 @@
     got = [swap(buf[cut:], *step) for buf, cut, step in zip(rest, cuts, steps[0])]
 
     qkv_total = qkv_tiles + width // tile + 1
-    qkv_parts = [(0, 4, zyxc[::-1]), (4, qkv_total, zxyc[::-1])]
+    qkv_parts = [(0, 6, zyxc[::-1]), (6, qkv_total, zxyc[::-1])]
     out_plans, shapes = scatter_plans(qkv_parts)
     g_input, *d_qkv = attend_backward(
         me, x, positions, ids, qkv, lse, gmixed, mid, d_norm, rest,
@@ -852,7 +852,7 @@
 
     qkv_buf = scatter_tiles(d_qkv, qkv_parts)
     mine = cut_parts(qkv_buf, qkv_parts)
-    low_left, low_left_t, low_right = low_bases(after(left_bases, qkv_buf), right_bases)
+    low_left, low_right = low_bases(after(left_bases, qkv_buf), right_bases)
     mine = [halve(buf, *step, low_left) for buf, step in zip(mine, steps[0])]
     for some in steps[1:]:
         rest = [halve(buf, *step, *mine) for buf, step in zip(rest, some)]
@@ -871,6 +871,7 @@
         jnp.where(owners[None, :] == jnp.arange(tiles)[:, None], jnp.arange(tiles)[None, :], 0), axis=1
     )
     sums = jnp.take(sums, tile_of, axis=0).reshape(reps, slots, rows, tile)
+    g_input = after(g_input, sums).astype(F32)
     small = small[: width // tile]
     near = []
     for k in range(reps):
@@ -885,13 +886,13 @@
     turned = right_turn(sums, low_right, seqs)
     small = after(small, turned)
     turned = lax.all_to_all(after(turned, g_input), "seq", 0, 0, tiled=True)
-    back = left_turns(turned, moments, low_left, low_left_t)
+    back = left_turns(turned, moments, low_left)
     news = last_turn(lax.all_to_all(back, "seq", 0, 0, tiled=True), low_right, *by_slot)
     first_new, second_new, new_weights = [values.transpose(1, 0, 2) for values in news]
 
     own = small[None]
-    for step in seq_bits:
-        own = double(own, *step, back)
+    for i, step in enumerate(seq_bits):
+        own = double(own, *step, *([turned] if i == 0 else [back]))
     masks = gather_masks(seq_bits)
     table = np.zeros(seqs, np.int32)
     for k, (i, _) in enumerate(masks):
@@ -906,7 +907,7 @@
     pos_first, pos_second, pos_dir = adam_step(grad_pos, pos_one, pos_two)
     return (
         result,
-        after(g_input, back).astype(F32),
+        g_input,
         first_new,
         second_new,
         new_weights,

time: 268 us -> 259 us (0.966)
  Pallas kernels: 73 us -> 66.5 us
  waiting for transfers between devices: 82.7 us -> 79.1 us
  starting transfers between devices: 70.7 us -> 74.1 us
    all_to_all x1, waiting for transfers between devices: 5.98 us -> 0.01 us  [body(): turned = lax.all_to_all(after(turned, g_input), 'seq', 0, 0, tiled=True)]
    ppermute x39, starting transfers between devices: 41.8 us -> 44.6 us  [swap(): return lax.ppermute(x, axis, [(i, i ^ bit) for i in range(size)])]
    unnamed x88 -> x92, local copies, waits for them, and re-layouts: 6.1 us -> 5.28 us
  transfers between devices with their start and end apart: 45 -> 45, of which waited for: 25 -> 25; matrix products, arithmetic and copies ran while one was open for 12% -> 11% of each run, Pallas kernels for 15% -> 14%
where the time goes in v1:
time: 259 us; the launch traced here: 258 us
  waiting for transfers between devices  79.1 us (31%)
  starting transfers between devices  74.1 us (29%)
  Pallas kernels  66.5 us (26%)
  other arithmetic  22.2 us (9%)
  local copies, waits for them, and re-layouts  14.7 us (6%)
    ppermute x39, waiting for transfers between devices, swap(): return lax.ppermute(x, axis, [(i, i ^ bit) for i in range(size)])  65.6 us
    ppermute x39, starting transfers between devices, swap(): return lax.ppermute(x, axis, [(i, i ^ bit) for i in range(size)])  44.6 us
    pallas_call x1, Pallas kernels, middle(): pl.pallas_call(functools.partial(middle_kernel, plans, out_plans, reps, r...  29 us
    all_to_all x4, starting transfers between devices, exchange(): return lax.all_to_all(x, axis, 0, 0, axis_index_groups=groups, tiled=True)  21.6 us
    pallas_call x1, Pallas kernels, attend_backward(): pl.pallas_call(functools.partial(attend_back_kernel, plans, out_plans, re...  14.8 us
    all_to_all x4, waiting for transfers between devices, exchange(): return lax.all_to_all(x, axis, 0, 0, axis_index_groups=groups, tiled=True)  9.74 us
    convert_element_type x13, other arithmetic, add(): return (a.astype(F32) + b.astype(F32)).astype(BF)  8.41 us
    pallas_call x1, Pallas kernels, attend_forward(): pl.pallas_call(functools.partial(attend_kernel, plans, reps), grid=(wins,...  7.46 us
  transfers between devices with their start and end apart: 45, of which 25 were waited for; matrix products, arithmetic and copies ran while one was open for 11% of the time, Pallas kernels for 14%

profile of v1, /device:TPU:0, one launch (start us, length us, event | category | flops | bytes accessed | tf_op | source)
XLA Modules:
  0.0 258.3 jit_solution(12082057819889425288)
XLA Ops:
  16.5 5.3 %all-to-all-start = ((bf16[16,64,512]{2,1,0:T(8,128)(2,1)}), bf16[16,64,512]{2,1,0:T(8,128)(2,1)S(1)}, u32[]{:S(2)}, u32[]{:S(2)}) async-start(bf16[16,64,512]{2,1,0:T(8,128)(2,1)} %param.19), calls=%async_computation | async-start | bytes 2097152 | tf_op jit(solution)/shard_map/all_to_all | solution.py:629
  30.7 5.2 %collective-permute-done.5 = bf16[4,4,16,256]{3,2,1,0:T(8,128)(2,1)S(1)} collective-permute-done((bf16[4,4,16,256]{3,2,1,0:T(8,128)(2,1)S(1)}, bf16[4,4,16,256]{3,2,1,0:T(8,128)(2,1)S(1)}, u32[]{:S(2)}, u32[]{:S(2)}) %collective-permute-start.5) | collective-permute-done | bytes 131104 | tf_op jit(solution)/shard_map/ppermute | solution.py:621
  37.1 7.9 %collective-permute-done.7 = bf16[2,18,16,256]{3,2,1,0:T(8,128)(2,1)S(1)} collective-permute-done((bf16[2,18,16,256]{3,2,1,0:T(8,128)(2,1)S(1)}, bf16[2,18,16,256]{3,2,1,0:T(8,128)(2,1)S(1)}, u32[]{:S(2)}, u32[]{:S(2)}) %collective-permute-start.7) | collective-permute-done | bytes 294944 | tf_op jit(solution)/shard_map/ppermute | solution.py:621
  48.7 4.1 %collective-permute-done.12 = bf16[4,9,16,256]{3,2,1,0:T(8,128)(2,1)S(1)} collective-permute-done((bf16[4,9,16,256]{3,2,1,0:T(8,128)(2,1)S(1)}, bf16[4,9,16,256]{3,2,1,0:T(8,128)(2,1)S(1)}, u32[]{:S(2)}, u32[]{:S(2)}) %collective-permute-start.12) | collective-permute-done | bytes 294944 | tf_op jit(solution)/shard_map/ppermute | solution.py:621
  58.6 6.8 %all-to-all-start.1 = ((bf16[16,64,512]{2,1,0:T(8,128)(2,1)}), bf16[16,64,512]{2,1,0:T(8,128)(2,1)}, u32[]{:S(2)}, u32[]{:S(2)}) async-start(bf16[16,64,512]{2,1,0:T(8,128)(2,1)} %param.20), calls=%async_computation.1 | async-start | bytes 2097152 | tf_op jit(solution)/shard_map/all_to_all | solution.py:629
  66.5 7.5 %attend_forward.1 = (bf16[2,512,1536]{2,1,0:T(8,128)(2,1)S(1)}, bf16[2,512,512]{2,1,0:T(8,128)(2,1)S(1)}, f32[2,8,512]{2,1,0:T(8,128)S(1)}) custom-call(s32[2]{0:T(128)S(1)} %pad_add_fusion.me_ref, bf16[8,2,64,512]{3,2,1,0:T(8,128)(2,1)S(1)} %bitcast.86, f32[512,512]{1,0:T(8,128)S(1)} %copy-done, s32[2,1,512]{2,1,0:T(1,128)S(1)} %broadcast_in_dim.77.ids_row, ...), custom_call_target="tpu_custom_call" | custom-call | flops 18000000 | tf_op jit(solution)/shard_map/attend_forward/pallas_call | solution.py:184
  82.0 9.7 %all-to-all-done.1 = bf16[16,64,512]{2,1,0:T(8,128)(2,1)} async-done(((bf16[16,64,512]{2,1,0:T(8,128)(2,1)}), bf16[16,64,512]{2,1,0:T(8,128)(2,1)}, u32[]{:S(2)}, u32[]{:S(2)}) %all-to-all-start.1) | async-done | bytes 1048608 | tf_op jit(solution)/shard_map/all_to_all | solution.py:629
  91.8 29.0 %middle.1 = (bf16[8,64,1408]{2,1,0:T(8,128)(2,1)}, f32[2,512,512]{2,1,0:T(8,128)}, bf16[2,512,512]{2,1,0:T(8,128)(2,1)}, f32[4,512]{1,0:T(4,128)}, bf16[288,16,2...) custom-call(s32[2]{0:T(128)} %copy-done.16, bf16[8,2,64,512]{3,2,1,0:T(8,128)(2,1)} %bitcast.87, f32[512,512]{1,0:T(8,128)} %pos_ref.5, ...), custom_call_target="tpu_custom_call" | custom-call | flops 27000000 | tf_op jit(solution)/shard_map/middle/pallas_call | solution.py:309
  120.8 4.5 %all-to-all-start.2 = ((bf16[8,64,1408]{2,1,0:T(8,128)(2,1)}), bf16[8,64,1408]{2,1,0:T(8,128)(2,1)}, u32[]{:S(2)}, u32[]{:S(2)}) async-start(bf16[8,64,1408]{2,1,0:T(8,128)(2,1)} %get-tuple-element.85), calls=%async_computation.2 | async-start | bytes 2883584 | tf_op jit(solution)/shard_map/all_to_all | solution.py:629
  125.7 3.2 %add_convert_fusion = bf16[288,16,256]{2,1,0:T(8,128)(2,1)S(1)} fusion(bf16[288,16,256]{2,1,0:T(8,128)(2,1)} %collective-permute-done.19, bf16[288,16,256]{2,1,0:T(8,128)(2,1)} %get-tuple-element.91), kind=kLoop, calls=%fused_computation.7 | loop fusion | flops 4718592 | bytes 7077888 | tf_op jit(solution)/shard_map/convert_element_type | solution.py:654
  132.3 14.8 %attend_backward.1 = (bf16[8,2,64,512]{3,2,1,0:T(8,128)(2,1)}, bf16[144,16,256]{2,1,0:T(8,128)(2,1)S(1)}, bf16[144,16,256]{2,1,0:T(8,128)(2,1)S(1)}) custom-call(s32[2]{0:T(128)S(1)} %copy-done.17, bf16[8,2,64,512]{3,2,1,0:T(8,128)(2,1)S(1)} %bitcast.88, f32[512,512]{1,0:T(8,128)S(1)} %copy-done.1, s32[2,1,512]{2,1,0:T(1,128)S(1)} %broadcast_in_dim.77.ids_row, ...), custom_call_target="tpu_custom_call" | custom-call | flops 22000000 | tf_op jit(solution)/shard_map/attend_backward/pallas_call | solution.py:460
  147.1 9.3 %collective-permute-done.21 = bf16[72,16,256]{2,1,0:T(8,128)(2,1)S(1)} collective-permute-done((bf16[72,16,256]{2,1,0:T(8,128)(2,1)S(1)}, bf16[72,16,256]{2,1,0:T(8,128)(2,1)S(1)}, u32[]{:S(2)}, u32[]{:S(2)}) %collective-permute-start.21) | collective-permute-done | bytes 589856 | tf_op jit(solution)/shard_map/ppermute | solution.py:621
  166.3 4.9 %all-to-all-start.3 = ((bf16[16,64,512]{2,1,0:T(8,128)(2,1)}), bf16[16,64,512]{2,1,0:T(8,128)(2,1)S(1)}, u32[]{:S(2)}, u32[]{:S(2)}) async-start(bf16[16,64,512]{2,1,0:T(8,128)(2,1)} %bitcast.21), calls=%async_computation.3 | async-start | bytes 2097152 | tf_op jit(solution)/shard_map/all_to_all | solution.py:629
  171.3 4.7 %low_bases.1 = (bf16[6,512,512]{2,1,0:T(8,128)(2,1)}, bf16[6,256,256]{2,1,0:T(8,128)(2,1)}) custom-call(f32[6,512,512]{2,1,0:T(8,128)} %left_ref, f32[6,256,256]{2,1,0:T(8,128)} %right_ref.1), custom_call_target="tpu_custom_call" | custom-call | flops 3000000 | tf_op jit(solution)/shard_map/low_bases/pallas_call | solution.py:604
  185.3 3.8 %collective-permute-done.24 = bf16[24,16,256]{2,1,0:T(8,128)(2,1)S(1)} collective-permute-done((bf16[24,16,256]{2,1,0:T(8,128)(2,1)S(1)}, bf16[24,16,256]{2,1,0:T(8,128)(2,1)S(1)}, u32[]{:S(2)}, u32[]{:S(2)}) %collective-permute-start.24) | collective-permute-done | bytes 196640 | tf_op jit(solution)/shard_map/ppermute | solution.py:621
  189.2 3.4 %collective-permute-start.29 = (bf16[2,9,16,256]{3,2,1,0:T(8,128)(2,1)S(1)}, bf16[2,9,16,256]{3,2,1,0:T(8,128)(2,1)S(1)}, u32[]{:S(2)}, u32[]{:S(2)}) collective-permute-start(bf16[2,9,16,256]{3,2,1,0:T(8,128)(2,1)S(1)} %fusion.3), channel_id=1, source_target_pairs={{0,8},{4,12},{8,0},{12,4},{16,24},{20,28},{24,16},{28,20},{1,9},{5... | collective-permute-start | bytes 442376 | tf_op jit(solution)/shard_map/ppermute | solution.py:621
  192.6 6.8 %collective-permute-done.30 = bf16[2,18,16,256]{3,2,1,0:T(8,128)(2,1)S(1)} collective-permute-done((bf16[2,18,16,256]{3,2,1,0:T(8,128)(2,1)S(1)}, bf16[2,18,16,256]{3,2,1,0:T(8,128)(2,1)S(1)}, u32[]{:S(2)}, u32[]{:S(2)}) %collective-permute-start.30) | collective-permute-done | bytes 294944 | tf_op jit(solution)/shard_map/ppermute | solution.py:621
  203.4 4.7 %collective-permute-done.32 = bf16[1,18,16,256]{3,2,1,0:T(8,128)(2,1)S(1)} collective-permute-done((bf16[1,18,16,256]{3,2,1,0:T(8,128)(2,1)S(1)}, bf16[1,18,16,256]{3,2,1,0:T(8,128)(2,1)S(1)}, u32[]{:S(2)}, u32[]{:S(2)}) %collective-permute-start.32) | collective-permute-done | bytes 147488 | tf_op jit(solution)/shard_map/ppermute | solution.py:621
  217.6 4.6 %all-to-all-start.4 = ((bf16[8,64,192]{2,1,0:T(8,128)(2,1)}), bf16[8,64,192]{2,1,0:T(8,128)(2,1)S(1)}, u32[]{:S(2)}, u32[]{:S(2)}) async-start(bf16[8,64,192]{2,1,0:T(8,128)(2,1)} %right_turn.1), calls=%async_computation.4 | async-start | bytes 524288 | tf_op jit(solution)/shard_map/all_to_all | solution.py:888
  223.5 3.0 %collective-permute-start.36 = (bf16[1,2,64,256]{3,2,1,0:T(8,128)(2,1)S(1)}, bf16[1,2,64,256]{3,2,1,0:T(8,128)(2,1)S(1)}, u32[]{:S(2)}, u32[]{:S(2)}) collective-permute-start(bf16[1,2,64,256]{3,2,1,0:T(8,128)(2,1)S(1)} %bitcast.104), channel_id=1, source_target_pairs={{0,16},{4,20},{8,24},{12,28},{16,0},{20,4},{24,8},{28,12},{1,17},{... | collective-permute-start | bytes 196616 | tf_op jit(solution)/shard_map/ppermute | solution.py:621
  227.5 6.7 %collective-permute-done.36 = bf16[1,2,64,256]{3,2,1,0:T(8,128)(2,1)S(1)} collective-permute-done((bf16[1,2,64,256]{3,2,1,0:T(8,128)(2,1)S(1)}, bf16[1,2,64,256]{3,2,1,0:T(8,128)(2,1)S(1)}, u32[]{:S(2)}, u32[]{:S(2)}) %collective-permute-start.36) | collective-permute-done | bytes 65568 | tf_op jit(solution)/shard_map/ppermute | solution.py:621
  234.9 5.4 %left_turns.1 = bf16[8,64,384]{2,1,0:T(8,128)(2,1)} custom-call(bf16[8,64,192]{2,1,0:T(8,128)(2,1)} %copy-done.36, bf16[8,64,1408]{2,1,0:T(8,128)(2,1)} %all-to-all-done.2.moments_ref, bf16[6,512,512]{2,1,0:T(8,128)(2,1)} %get-tuple-element.101.left_ref), custom_call_target="tpu_custom_call" | custom-call | flops 3000000 | tf_op jit(solution)/shard_map/left_turns/pallas_call | solution.py:532
  242.6 3.5 %all-to-all-start.5 = ((bf16[8,64,384]{2,1,0:T(8,128)(2,1)}), bf16[8,64,384]{2,1,0:T(8,128)(2,1)S(1)}, u32[]{:S(2)}, u32[]{:S(2)}) async-start(bf16[8,64,384]{2,1,0:T(8,128)(2,1)} %left_turns.1), calls=%async_computation.5 | async-start | bytes 786432 | tf_op jit(solution)/shard_map/all_to_all | solution.py:890
  253.2 3.7 %all-to-all-done.5.back_ref = bf16[8,64,384]{2,1,0:T(8,128)(2,1)S(1)} async-done(((bf16[8,64,384]{2,1,0:T(8,128)(2,1)}), bf16[8,64,384]{2,1,0:T(8,128)(2,1)S(1)}, u32[]{:S(2)}, u32[]{:S(2)}) %all-to-all-start.5) | async-done | bytes 393248 | tf_op jit(solution)/shard_map/all_to_all | solution.py:890
  (276 shorter events, 94.3 us)
Async XLA Ops:
  14.5 9.8 %collective-permute-start.6 = (bf16[1,18,16,256]{3,2,1,0:T(8,128)(2,1)S(1)}, bf16[1,18,16,256]{3,2,1,0:T(8,128)(2,1)S(1)}, u32[]{:S(2)}, u32[]{:S(2)}) collective-permute-start(bf16[1,18,16,256]{3,2,1,0:T(8,128)(2,1)S(1)} %slice_bitcast_fusion), channel_id=1, source_target_pairs={{0,16},{4,20},{8,24},{12,28},{16,0},{20,4},{24,8},{28,12},{1,17},{... | collective-permute-start | bytes 442376 | tf_op jit(solution)/shard_map/ppermute | solution.py:621
  15.7 8.7 %collective-permute-start.4 = (bf16[2,7,16,256]{3,2,1,0:T(8,128)(2,1)S(1)}, bf16[2,7,16,256]{3,2,1,0:T(8,128)(2,1)S(1)}, u32[]{:S(2)}, u32[]{:S(2)}) collective-permute-start(bf16[2,7,16,256]{3,2,1,0:T(8,128)(2,1)S(1)} %pad_maximum_fusion.24), channel_id=1, source_target_pairs={{0,8},{4,12},{8,0},{12,4},{16,24},{20,28},{24,16},{28,20},{1,9},{5... | collective-permute-start | bytes 344072 | tf_op jit(solution)/shard_map/ppermute | solution.py:621
  16.5 42.1 %all-to-all-start = ((bf16[16,64,512]{2,1,0:T(8,128)(2,1)}), bf16[16,64,512]{2,1,0:T(8,128)(2,1)S(1)}, u32[]{:S(2)}, u32[]{:S(2)}) async-start(bf16[16,64,512]{2,1,0:T(8,128)(2,1)} %param.19), calls=%async_computation | async-start | bytes 2097152 | tf_op jit(solution)/shard_map/all_to_all | solution.py:629
  24.3 20.7 %collective-permute-start.7 = (bf16[2,18,16,256]{3,2,1,0:T(8,128)(2,1)S(1)}, bf16[2,18,16,256]{3,2,1,0:T(8,128)(2,1)S(1)}, u32[]{:S(2)}, u32[]{:S(2)}) collective-permute-start(bf16[2,18,16,256]{3,2,1,0:T(8,128)(2,1)S(1)} %pad_maximum_fusion.12), channel_id=1, source_target_pairs={{0,8},{4,12},{8,0},{12,4},{16,24},{20,28},{24,16},{28,20},{1,9},{5... | collective-permute-start | bytes 884744 | tf_op jit(solution)/shard_map/ppermute | solution.py:621
  25.6 10.3 %collective-permute-start.5 = (bf16[4,4,16,256]{3,2,1,0:T(8,128)(2,1)S(1)}, bf16[4,4,16,256]{3,2,1,0:T(8,128)(2,1)S(1)}, u32[]{:S(2)}, u32[]{:S(2)}) collective-permute-start(bf16[4,4,16,256]{3,2,1,0:T(8,128)(2,1)S(1)} %slice.230), channel_id=1, source_target_pairs={{0,4},{4,0},{8,12},{12,8},{16,20},{20,16},{24,28},{28,24},{1,5},{5... | collective-permute-start | bytes 393224 | tf_op jit(solution)/shard_map/ppermute | solution.py:621
  29.2 19.4 %collective-permute-start.11 = (bf16[8,3,16,256]{3,2,1,0:T(8,128)(2,1)S(1)}, bf16[8,3,16,256]{3,2,1,0:T(8,128)(2,1)S(1)}, u32[]{:S(2)}, u32[]{:S(2)}) collective-permute-start(bf16[8,3,16,256]{3,2,1,0:T(8,128)(2,1)S(1)} %pad_maximum_fusion.17), channel_id=1, source_target_pairs={{0,4},{4,0},{8,12},{12,8},{16,20},{20,16},{24,28},{28,24},{1,5},{5... | collective-permute-start | bytes 589832 | tf_op jit(solution)/shard_map/ppermute | solution.py:621
  36.0 12.6 %collective-permute-start.10 = (bf16[8,4,16,256]{3,2,1,0:T(8,128)(2,1)S(1)}, bf16[8,4,16,256]{3,2,1,0:T(8,128)(2,1)S(1)}, u32[]{:S(2)}, u32[]{:S(2)}) collective-permute-start(bf16[8,4,16,256]{3,2,1,0:T(8,128)(2,1)S(1)} %pad_maximum_fusion.10), channel_id=1, source_target_pairs={{0,2},{1,3},{2,0},{3,1},{4,6},{5,7},{6,4},{7,5},{8,10},{9,11},{10,... | collective-permute-start | bytes 786440 | tf_op jit(solution)/shard_map/ppermute | solution.py:621
  48.6 17.8 %collective-permute-start.13 = (bf16[16,4,16,256]{3,2,1,0:T(8,128)(2,1)S(1)}, bf16[16,4,16,256]{3,2,1,0:T(8,128)(2,1)}, u32[]{:S(2)}, u32[]{:S(2)}) collective-permute-start(bf16[16,4,16,256]{3,2,1,0:T(8,128)(2,1)S(1)} %pad_maximum_fusion.6.refs_0_), channel_id=1, source_target_pairs={{0,1},{1,0},{2,3},{3,2},{4,5},{5,4},{6,7},{7,6},{8,9},{9,8},{10,11... | collective-permute-start | bytes 1572872 | tf_op jit(solution)/shard_map/ppermute | solution.py:621
  54.8 20.9 %collective-permute-start.16 = (bf16[8,9,16,256]{3,2,1,0:T(8,128)(2,1)}, bf16[8,9,16,256]{3,2,1,0:T(8,128)(2,1)}, u32[]{:S(2)}, u32[]{:S(2)}) collective-permute-start(bf16[8,9,16,256]{3,2,1,0:T(8,128)(2,1)} %pad_maximum_fusion.5), channel_id=1, source_target_pairs={{0,4},{4,0},{8,12},{12,8},{16,20},{20,16},{24,28},{28,24},{1,5},{5... | collective-permute-start | bytes 1769480 | tf_op jit(solution)/shard_map/ppermute | solution.py:621
  57.4 18.3 %collective-permute-start.15 = (bf16[8,9,16,256]{3,2,1,0:T(8,128)(2,1)}, bf16[8,9,16,256]{3,2,1,0:T(8,128)(2,1)}, u32[]{:S(2)}, u32[]{:S(2)}) collective-permute-start(bf16[8,9,16,256]{3,2,1,0:T(8,128)(2,1)} %pad_maximum_fusion.4), channel_id=1, source_target_pairs={{0,2},{1,3},{2,0},{3,1},{4,6},{5,7},{6,4},{7,5},{8,10},{9,11},{10,... | collective-permute-start | bytes 1769480 | tf_op jit(solution)/shard_map/ppermute | solution.py:621
  58.6 33.1 %all-to-all-start.1 = ((bf16[16,64,512]{2,1,0:T(8,128)(2,1)}), bf16[16,64,512]{2,1,0:T(8,128)(2,1)}, u32[]{:S(2)}, u32[]{:S(2)}) async-start(bf16[16,64,512]{2,1,0:T(8,128)(2,1)} %param.20), calls=%async_computation.1 | async-start | bytes 2097152 | tf_op jit(solution)/shard_map/all_to_all | solution.py:629
  120.8 45.5 %all-to-all-start.2 = ((bf16[8,64,1408]{2,1,0:T(8,128)(2,1)}), bf16[8,64,1408]{2,1,0:T(8,128)(2,1)}, u32[]{:S(2)}, u32[]{:S(2)}) async-start(bf16[8,64,1408]{2,1,0:T(8,128)(2,1)} %get-tuple-element.85), calls=%async_computation.2 | async-start | bytes 2883584 | tf_op jit(solution)/shard_map/all_to_all | solution.py:629
  129.0 18.1 %collective-permute-start.20 = (bf16[72,16,256]{2,1,0:T(8,128)(2,1)S(1)}, bf16[72,16,256]{2,1,0:T(8,128)(2,1)S(1)}, u32[]{:S(2)}, u32[]{:S(2)}) collective-permute-start(bf16[72,16,256]{2,1,0:T(8,128)(2,1)S(1)} %get-tuple-element.135), channel_id=1, source_target_pairs={{0,2},{1,3},{2,0},{3,1},{4,6},{5,7},{6,4},{7,5},{8,10},{9,11},{10,... | collective-permute-start | bytes 1769480 | tf_op jit(solution)/shard_map/ppermute | solution.py:621
  130.4 26.0 %collective-permute-start.21 = (bf16[72,16,256]{2,1,0:T(8,128)(2,1)S(1)}, bf16[72,16,256]{2,1,0:T(8,128)(2,1)S(1)}, u32[]{:S(2)}, u32[]{:S(2)}) collective-permute-start(bf16[72,16,256]{2,1,0:T(8,128)(2,1)S(1)} %get-tuple-element.134), channel_id=1, source_target_pairs={{0,4},{4,0},{8,12},{12,8},{16,20},{20,16},{24,28},{28,24},{1,5},{5... | collective-permute-start | bytes 1769480 | tf_op jit(solution)/shard_map/ppermute | solution.py:621
  160.4 15.6 %collective-permute-start.26 = (bf16[24,16,256]{2,1,0:T(8,128)(2,1)S(1)}, bf16[24,16,256]{2,1,0:T(8,128)(2,1)}, u32[]{:S(2)}, u32[]{:S(2)}) collective-permute-start(bf16[24,16,256]{2,1,0:T(8,128)(2,1)S(1)} %slice.252), channel_id=1, source_target_pairs={{0,4},{4,0},{8,12},{12,8},{16,20},{20,16},{24,28},{28,24},{1,5},{5... | collective-permute-start | bytes 589832 | tf_op jit(solution)/shard_map/ppermute | solution.py:621
  160.4 17.7 %collective-permute-start.23 = (bf16[48,16,256]{2,1,0:T(8,128)(2,1)}, bf16[48,16,256]{2,1,0:T(8,128)(2,1)}, u32[]{:S(2)}, u32[]{:S(2)}) collective-permute-start(bf16[48,16,256]{2,1,0:T(8,128)(2,1)} %slice.245), channel_id=1, source_target_pairs={{0,2},{1,3},{2,0},{3,1},{4,6},{5,7},{6,4},{7,5},{8,10},{9,11},{10,... | collective-permute-start | bytes 1179656 | tf_op jit(solution)/shard_map/ppermute | solution.py:621
  162.8 16.3 %collective-permute-start.25 = (bf16[36,16,256]{2,1,0:T(8,128)(2,1)}, bf16[36,16,256]{2,1,0:T(8,128)(2,1)}, u32[]{:S(2)}, u32[]{:S(2)}) collective-permute-start(bf16[36,16,256]{2,1,0:T(8,128)(2,1)} %slice.250), channel_id=1, source_target_pairs={{0,4},{4,0},{8,12},{12,8},{16,20},{20,16},{24,28},{28,24},{1,5},{5... | collective-permute-start | bytes 884744 | tf_op jit(solution)/shard_map/ppermute | solution.py:621
  165.6 14.7 %collective-permute-start.27 = (bf16[36,16,256]{2,1,0:T(8,128)(2,1)}, bf16[36,16,256]{2,1,0:T(8,128)(2,1)}, u32[]{:S(2)}, u32[]{:S(2)}) collective-permute-start(bf16[36,16,256]{2,1,0:T(8,128)(2,1)} %slice.255), channel_id=1, source_target_pairs={{0,2},{1,3},{2,0},{3,1},{4,6},{5,7},{6,4},{7,5},{8,10},{9,11},{10,... | collective-permute-start | bytes 884744 | tf_op jit(solution)/shard_map/ppermute | solution.py:621
  166.3 45.3 %all-to-all-start.3 = ((bf16[16,64,512]{2,1,0:T(8,128)(2,1)}), bf16[16,64,512]{2,1,0:T(8,128)(2,1)S(1)}, u32[]{:S(2)}, u32[]{:S(2)}) async-start(bf16[16,64,512]{2,1,0:T(8,128)(2,1)} %bitcast.21), calls=%async_computation.3 | async-start | bytes 2097152 | tf_op jit(solution)/shard_map/all_to_all | solution.py:629
  183.8 15.6 %collective-permute-start.30 = (bf16[2,18,16,256]{3,2,1,0:T(8,128)(2,1)S(1)}, bf16[2,18,16,256]{3,2,1,0:T(8,128)(2,1)S(1)}, u32[]{:S(2)}, u32[]{:S(2)}) collective-permute-start(bf16[2,18,16,256]{3,2,1,0:T(8,128)(2,1)S(1)} %pad_maximum_fusion.11), channel_id=1, source_target_pairs={{0,8},{4,12},{8,0},{12,4},{16,24},{20,28},{24,16},{28,20},{1,9},{5... | collective-permute-start | bytes 884744 | tf_op jit(solution)/shard_map/ppermute | solution.py:621
  189.2 11.7 %collective-permute-start.29 = (bf16[2,9,16,256]{3,2,1,0:T(8,128)(2,1)S(1)}, bf16[2,9,16,256]{3,2,1,0:T(8,128)(2,1)S(1)}, u32[]{:S(2)}, u32[]{:S(2)}) collective-permute-start(bf16[2,9,16,256]{3,2,1,0:T(8,128)(2,1)S(1)} %fusion.3), channel_id=1, source_target_pairs={{0,8},{4,12},{8,0},{12,4},{16,24},{20,28},{24,16},{28,20},{1,9},{5... | collective-permute-start | bytes 442376 | tf_op jit(solution)/shard_map/ppermute | solution.py:621
  217.6 16.6 %all-to-all-start.4 = ((bf16[8,64,192]{2,1,0:T(8,128)(2,1)}), bf16[8,64,192]{2,1,0:T(8,128)(2,1)S(1)}, u32[]{:S(2)}, u32[]{:S(2)}) async-start(bf16[8,64,192]{2,1,0:T(8,128)(2,1)} %right_turn.1), calls=%async_computation.4 | async-start | bytes 524288 | tf_op jit(solution)/shard_map/all_to_all | solution.py:888
  223.5 10.8 %collective-permute-start.36 = (bf16[1,2,64,256]{3,2,1,0:T(8,128)(2,1)S(1)}, bf16[1,2,64,256]{3,2,1,0:T(8,128)(2,1)S(1)}, u32[]{:S(2)}, u32[]{:S(2)}) collective-permute-start(bf16[1,2,64,256]{3,2,1,0:T(8,128)(2,1)S(1)} %bitcast.104), channel_id=1, source_target_pairs={{0,16},{4,20},{8,24},{12,28},{16,0},{20,4},{24,8},{28,12},{1,17},{... | collective-permute-start | bytes 196616 | tf_op jit(solution)/shard_map/ppermute | solution.py:621
  242.6 14.3 %all-to-all-start.5 = ((bf16[8,64,384]{2,1,0:T(8,128)(2,1)}), bf16[8,64,384]{2,1,0:T(8,128)(2,1)S(1)}, u32[]{:S(2)}, u32[]{:S(2)}) async-start(bf16[8,64,384]{2,1,0:T(8,128)(2,1)} %left_turns.1), calls=%async_computation.5 | async-start | bytes 786432 | tf_op jit(solution)/shard_map/all_to_all | solution.py:890
  (66 other events, 382.9 us)

commit v2 on v1

--- a/solution.py
+++ b/solution.py
@@ -203,7 +203,7 @@
             jax.ShapeDtypeStruct((wins, H, win), F32),
         ],
         scratch_shapes=[pltpu.VMEM((win, win), F32), pltpu.VMEM((tiles, width, tile), BF)],
-        compiler_params=memory(32),
+        compiler_params=memory(28),
         cost_estimate=takes(18),
         name="attend_forward",
     )(me, x, positions, ids[:, None, :], ids[:, :, None], *w)
@@ -244,12 +244,11 @@
     for t in range(ups):
         pre = nn(low, w_ref[up + t])
         square = pre * pre
-        bent = jnp.tanh(GELU_A * pre * (1.0 + GELU_B * square))
-        act[:, t * tile : (t + 1) * tile] = (0.5 * pre * (1.0 + bent)).astype(BF)
-        slope[:, t * tile : (t + 1) * tile] = (
-            0.5 * (1.0 + bent)
-            + 0.5 * pre * (1.0 - bent * bent) * (GELU_A + 3.0 * GELU_A * GELU_B * square)
-        ).astype(BF)
+        lifted = 1.0 + jnp.tanh(pre * (GELU_A + GELU_A * GELU_B * square))
+        halved = 0.5 * pre
+        steep = halved * (GELU_A + 3.0 * GELU_A * GELU_B * square)
+        act[:, t * tile : (t + 1) * tile] = (halved * lifted).astype(BF)
+        slope[:, t * tile : (t + 1) * tile] = (lifted * (0.5 + steep * (2.0 - lifted))).astype(BF)
     branch = jnp.concatenate(
         [
             sum(nn(act[:, b * width : (b + 1) * width], w_ref[down + 2 * b + j]) for b in range(blocks))
@@ -483,7 +482,7 @@
             pltpu.VMEM((tiles, width, tile), BF),
             pltpu.VMEM((tiles + width // tile + 1, width, tile), F32),
         ],
-        compiler_params=memory(36),
+        compiler_params=memory(30),
         cost_estimate=takes(22),
         name="attend_backward",
     )(me, x, positions, ids[:, None, :], ids[:, :, None], qkv, lse, gmixed, mid, dnorm, *w, *behind)
@@ -813,7 +812,6 @@
 
     zyxc = seq_bits + far_bits + core_bit
     zxyc = seq_bits[:-1] + far_bits + seq_bits[-1:] + core_bit
-    ids = after(ids, *rest)
     ahead = attend_forward(me, x, positions, ids, w_qkv, qkv_plans, qkv_tiles, tile, reps)
     for i in range(1, len(orders[0])):
         got = [swap(buf, *order[i]) for buf, order in zip(rest, orders)]

time: 259 us -> 258 us (level)
  transfers between devices with their start and end apart: 45 -> 45, of which waited for: 25 -> 24; matrix products, arithmetic and copies ran while one was open for 11% -> 11% of each run, Pallas kernels for 14% -> 14%
where the time goes in v2:
time: 258 us; the launch traced here: 257 us
  waiting for transfers between devices  78.3 us (30%)
  starting transfers between devices  73.9 us (29%)
  Pallas kernels  65.9 us (26%)
  other arithmetic  22.2 us (9%)
  local copies, waits for them, and re-layouts  15.2 us (6%)
    ppermute x39, waiting for transfers between devices, swap(): return lax.ppermute(x, axis, [(i, i ^ bit) for i in range(size)])  65.1 us
    ppermute x39, starting transfers between devices, swap(): return lax.ppermute(x, axis, [(i, i ^ bit) for i in range(size)])  44.2 us
    pallas_call x1, Pallas kernels, middle(): pl.pallas_call(functools.partial(middle_kernel, plans, out_plans, reps, r...  28.4 us
    all_to_all x4, starting transfers between devices, exchange(): return lax.all_to_all(x, axis, 0, 0, axis_index_groups=groups, tiled=True)  21.6 us
    pallas_call x1, Pallas kernels, attend_backward(): pl.pallas_call(functools.partial(attend_back_kernel, plans, out_plans, re...  14.8 us
    all_to_all x4, waiting for transfers between devices, exchange(): return lax.all_to_all(x, axis, 0, 0, axis_index_groups=groups, tiled=True)  9.54 us
    convert_element_type x13, other arithmetic, add(): return (a.astype(F32) + b.astype(F32)).astype(BF)  8.41 us
    pallas_call x1, Pallas kernels, attend_forward(): pl.pallas_call(functools.partial(attend_kernel, plans, reps), grid=(wins,...  7.45 us
  transfers between devices with their start and end apart: 45, of which 24 were waited for; matrix products, arithmetic and copies ran while one was open for 11% of the time, Pallas kernels for 14%

profile of v2, /device:TPU:0, one launch (start us, length us, event | category | flops | bytes accessed | tf_op | source)
XLA Modules:
  0.0 257.2 jit_solution(15776795326470368835)
XLA Ops:
  16.5 5.3 %all-to-all-start = ((bf16[16,64,512]{2,1,0:T(8,128)(2,1)}), bf16[16,64,512]{2,1,0:T(8,128)(2,1)S(1)}, u32[]{:S(2)}, u32[]{:S(2)}) async-start(bf16[16,64,512]{2,1,0:T(8,128)(2,1)} %param.19), calls=%async_computation | async-start | bytes 2097152 | tf_op jit(solution)/shard_map/all_to_all | solution.py:628
  30.7 5.2 %collective-permute-done.5 = bf16[4,4,16,256]{3,2,1,0:T(8,128)(2,1)S(1)} collective-permute-done((bf16[4,4,16,256]{3,2,1,0:T(8,128)(2,1)S(1)}, bf16[4,4,16,256]{3,2,1,0:T(8,128)(2,1)S(1)}, u32[]{:S(2)}, u32[]{:S(2)}) %collective-permute-start.5) | collective-permute-done | bytes 131104 | tf_op jit(solution)/shard_map/ppermute | solution.py:620
  37.1 7.9 %collective-permute-done.12 = bf16[2,18,16,256]{3,2,1,0:T(8,128)(2,1)S(1)} collective-permute-done((bf16[2,18,16,256]{3,2,1,0:T(8,128)(2,1)S(1)}, bf16[2,18,16,256]{3,2,1,0:T(8,128)(2,1)S(1)}, u32[]{:S(2)}, u32[]{:S(2)}) %collective-permute-start.12) | collective-permute-done | bytes 294944 | tf_op jit(solution)/shard_map/ppermute | solution.py:620
  48.8 4.1 %collective-permute-done.15 = bf16[4,9,16,256]{3,2,1,0:T(8,128)(2,1)S(1)} collective-permute-done((bf16[4,9,16,256]{3,2,1,0:T(8,128)(2,1)S(1)}, bf16[4,9,16,256]{3,2,1,0:T(8,128)(2,1)S(1)}, u32[]{:S(2)}, u32[]{:S(2)}) %collective-permute-start.15) | collective-permute-done | bytes 294944 | tf_op jit(solution)/shard_map/ppermute | solution.py:620
  57.8 7.1 %all-to-all-start.1 = ((bf16[16,64,512]{2,1,0:T(8,128)(2,1)}), bf16[16,64,512]{2,1,0:T(8,128)(2,1)}, u32[]{:S(2)}, u32[]{:S(2)}) async-start(bf16[16,64,512]{2,1,0:T(8,128)(2,1)} %param.20), calls=%async_computation.1 | async-start | bytes 2097152 | tf_op jit(solution)/shard_map/all_to_all | solution.py:628
  66.3 7.5 %attend_forward.1 = (bf16[2,512,1536]{2,1,0:T(8,128)(2,1)S(1)}, bf16[2,512,512]{2,1,0:T(8,128)(2,1)S(1)}, f32[2,8,512]{2,1,0:T(8,128)S(1)}) custom-call(s32[2]{0:T(128)S(1)} %pad_add_fusion.me_ref, bf16[8,2,64,512]{3,2,1,0:T(8,128)(2,1)S(1)} %bitcast.85, f32[512,512]{1,0:T(8,128)S(1)} %copy-done, s32[2,1,512]{2,1,0:T(1,128)S(1)} %broadcast_in_dim_reshape.8.ids_row, ...), custom_call_target="tpu_custom_call" | custom-call | flops 18000000 | tf_op jit(solution)/shard_map/attend_forward/pallas_call | solution.py:184
  81.8 9.5 %all-to-all-done.1 = bf16[16,64,512]{2,1,0:T(8,128)(2,1)} async-done(((bf16[16,64,512]{2,1,0:T(8,128)(2,1)}), bf16[16,64,512]{2,1,0:T(8,128)(2,1)}, u32[]{:S(2)}, u32[]{:S(2)}) %all-to-all-start.1) | async-done | bytes 1048608 | tf_op jit(solution)/shard_map/all_to_all | solution.py:628
  91.3 28.4 %middle.1 = (bf16[8,64,1408]{2,1,0:T(8,128)(2,1)}, f32[2,512,512]{2,1,0:T(8,128)}, bf16[2,512,512]{2,1,0:T(8,128)(2,1)}, f32[4,512]{1,0:T(4,128)}, bf16[288,16,2...) custom-call(s32[2]{0:T(128)} %copy-done.16, bf16[8,2,64,512]{3,2,1,0:T(8,128)(2,1)} %bitcast.86, f32[512,512]{1,0:T(8,128)} %pos_ref.5, ...), custom_call_target="tpu_custom_call" | custom-call | flops 27000000 | tf_op jit(solution)/shard_map/middle/pallas_call | solution.py:308
  119.8 4.5 %all-to-all-start.2 = ((bf16[8,64,1408]{2,1,0:T(8,128)(2,1)}), bf16[8,64,1408]{2,1,0:T(8,128)(2,1)}, u32[]{:S(2)}, u32[]{:S(2)}) async-start(bf16[8,64,1408]{2,1,0:T(8,128)(2,1)} %get-tuple-element.83), calls=%async_computation.2 | async-start | bytes 2883584 | tf_op jit(solution)/shard_map/all_to_all | solution.py:628
  124.7 3.2 %add_convert_fusion = bf16[288,16,256]{2,1,0:T(8,128)(2,1)S(1)} fusion(bf16[288,16,256]{2,1,0:T(8,128)(2,1)} %collective-permute-done.19, bf16[288,16,256]{2,1,0:T(8,128)(2,1)} %get-tuple-element.89), kind=kLoop, calls=%fused_computation.7 | loop fusion | flops 4718592 | bytes 7077888 | tf_op jit(solution)/shard_map/convert_element_type | solution.py:653
  130.9 14.8 %attend_backward.1 = (bf16[8,2,64,512]{3,2,1,0:T(8,128)(2,1)}, bf16[144,16,256]{2,1,0:T(8,128)(2,1)S(1)}, bf16[144,16,256]{2,1,0:T(8,128)(2,1)S(1)}) custom-call(s32[2]{0:T(128)S(1)} %copy-done.17, bf16[8,2,64,512]{3,2,1,0:T(8,128)(2,1)S(1)} %bitcast.87, f32[512,512]{1,0:T(8,128)S(1)} %copy-done.1, s32[2,1,512]{2,1,0:T(1,128)S(1)} %broadcast_in_dim_reshape.8.ids_row, ...), custom_call_target="tpu_custom_call" | custom-call | flops 22000000 | tf_op jit(solution)/shard_map/attend_backward/pallas_call | solution.py:459
  145.7 9.7 %collective-permute-done.21 = bf16[72,16,256]{2,1,0:T(8,128)(2,1)S(1)} collective-permute-done((bf16[72,16,256]{2,1,0:T(8,128)(2,1)S(1)}, bf16[72,16,256]{2,1,0:T(8,128)(2,1)S(1)}, u32[]{:S(2)}, u32[]{:S(2)}) %collective-permute-start.21) | collective-permute-done | bytes 589856 | tf_op jit(solution)/shard_map/ppermute | solution.py:620
  165.3 4.6 %all-to-all-start.3 = ((bf16[16,64,512]{2,1,0:T(8,128)(2,1)}), bf16[16,64,512]{2,1,0:T(8,128)(2,1)S(1)}, u32[]{:S(2)}, u32[]{:S(2)}) async-start(bf16[16,64,512]{2,1,0:T(8,128)(2,1)} %bitcast.20), calls=%async_computation.3 | async-start | bytes 2097152 | tf_op jit(solution)/shard_map/all_to_all | solution.py:628
  169.9 4.7 %low_bases.1 = (bf16[6,512,512]{2,1,0:T(8,128)(2,1)}, bf16[6,256,256]{2,1,0:T(8,128)(2,1)}) custom-call(f32[6,512,512]{2,1,0:T(8,128)} %left_ref, f32[6,256,256]{2,1,0:T(8,128)} %right_ref.1), custom_call_target="tpu_custom_call" | custom-call | flops 3000000 | tf_op jit(solution)/shard_map/low_bases/pallas_call | solution.py:603
  184.0 3.8 %collective-permute-done.24 = bf16[24,16,256]{2,1,0:T(8,128)(2,1)S(1)} collective-permute-done((bf16[24,16,256]{2,1,0:T(8,128)(2,1)S(1)}, bf16[24,16,256]{2,1,0:T(8,128)(2,1)S(1)}, u32[]{:S(2)}, u32[]{:S(2)}) %collective-permute-start.24) | collective-permute-done | bytes 196640 | tf_op jit(solution)/shard_map/ppermute | solution.py:620
  187.9 3.4 %collective-permute-start.29 = (bf16[2,9,16,256]{3,2,1,0:T(8,128)(2,1)S(1)}, bf16[2,9,16,256]{3,2,1,0:T(8,128)(2,1)S(1)}, u32[]{:S(2)}, u32[]{:S(2)}) collective-permute-start(bf16[2,9,16,256]{3,2,1,0:T(8,128)(2,1)S(1)} %fusion.3), channel_id=1, source_target_pairs={{0,8},{4,12},{8,0},{12,4},{16,24},{20,28},{24,16},{28,20},{1,9},{5... | collective-permute-start | bytes 442376 | tf_op jit(solution)/shard_map/ppermute | solution.py:620
  191.3 6.9 %collective-permute-done.30 = bf16[2,18,16,256]{3,2,1,0:T(8,128)(2,1)S(1)} collective-permute-done((bf16[2,18,16,256]{3,2,1,0:T(8,128)(2,1)S(1)}, bf16[2,18,16,256]{3,2,1,0:T(8,128)(2,1)S(1)}, u32[]{:S(2)}, u32[]{:S(2)}) %collective-permute-start.30) | collective-permute-done | bytes 294944 | tf_op jit(solution)/shard_map/ppermute | solution.py:620
  202.1 4.7 %collective-permute-done.32 = bf16[1,18,16,256]{3,2,1,0:T(8,128)(2,1)S(1)} collective-permute-done((bf16[1,18,16,256]{3,2,1,0:T(8,128)(2,1)S(1)}, bf16[1,18,16,256]{3,2,1,0:T(8,128)(2,1)S(1)}, u32[]{:S(2)}, u32[]{:S(2)}) %collective-permute-start.32) | collective-permute-done | bytes 147488 | tf_op jit(solution)/shard_map/ppermute | solution.py:620
  216.3 4.7 %all-to-all-start.4 = ((bf16[8,64,192]{2,1,0:T(8,128)(2,1)}), bf16[8,64,192]{2,1,0:T(8,128)(2,1)S(1)}, u32[]{:S(2)}, u32[]{:S(2)}) async-start(bf16[8,64,192]{2,1,0:T(8,128)(2,1)} %right_turn.1), calls=%async_computation.4 | async-start | bytes 524288 | tf_op jit(solution)/shard_map/all_to_all | solution.py:886
  222.3 3.0 %collective-permute-start.36 = (bf16[1,2,64,256]{3,2,1,0:T(8,128)(2,1)S(1)}, bf16[1,2,64,256]{3,2,1,0:T(8,128)(2,1)S(1)}, u32[]{:S(2)}, u32[]{:S(2)}) collective-permute-start(bf16[1,2,64,256]{3,2,1,0:T(8,128)(2,1)S(1)} %bitcast.103), channel_id=1, source_target_pairs={{0,16},{4,20},{8,24},{12,28},{16,0},{20,4},{24,8},{28,12},{1,17},{... | collective-permute-start | bytes 196616 | tf_op jit(solution)/shard_map/ppermute | solution.py:620
  226.3 6.8 %collective-permute-done.36 = bf16[1,2,64,256]{3,2,1,0:T(8,128)(2,1)S(1)} collective-permute-done((bf16[1,2,64,256]{3,2,1,0:T(8,128)(2,1)S(1)}, bf16[1,2,64,256]{3,2,1,0:T(8,128)(2,1)S(1)}, u32[]{:S(2)}, u32[]{:S(2)}) %collective-permute-start.36) | collective-permute-done | bytes 65568 | tf_op jit(solution)/shard_map/ppermute | solution.py:620
  233.8 5.4 %left_turns.1 = bf16[8,64,384]{2,1,0:T(8,128)(2,1)} custom-call(bf16[8,64,192]{2,1,0:T(8,128)(2,1)} %copy-done.36, bf16[8,64,1408]{2,1,0:T(8,128)(2,1)} %all-to-all-done.2.moments_ref, bf16[6,512,512]{2,1,0:T(8,128)(2,1)} %get-tuple-element.99.left_ref), custom_call_target="tpu_custom_call" | custom-call | flops 3000000 | tf_op jit(solution)/shard_map/left_turns/pallas_call | solution.py:531
  241.4 3.5 %all-to-all-start.5 = ((bf16[8,64,384]{2,1,0:T(8,128)(2,1)}), bf16[8,64,384]{2,1,0:T(8,128)(2,1)S(1)}, u32[]{:S(2)}, u32[]{:S(2)}) async-start(bf16[8,64,384]{2,1,0:T(8,128)(2,1)} %left_turns.1), calls=%async_computation.5 | async-start | bytes 786432 | tf_op jit(solution)/shard_map/all_to_all | solution.py:888
  252.1 3.7 %all-to-all-done.5.back_ref = bf16[8,64,384]{2,1,0:T(8,128)(2,1)S(1)} async-done(((bf16[8,64,384]{2,1,0:T(8,128)(2,1)}), bf16[8,64,384]{2,1,0:T(8,128)(2,1)S(1)}, u32[]{:S(2)}, u32[]{:S(2)}) %all-to-all-start.5) | async-done | bytes 393248 | tf_op jit(solution)/shard_map/all_to_all | solution.py:888
  (275 shorter events, 93.4 us)
Async XLA Ops:
  14.5 9.8 %collective-permute-start.11 = (bf16[1,18,16,256]{3,2,1,0:T(8,128)(2,1)S(1)}, bf16[1,18,16,256]{3,2,1,0:T(8,128)(2,1)S(1)}, u32[]{:S(2)}, u32[]{:S(2)}) collective-permute-start(bf16[1,18,16,256]{3,2,1,0:T(8,128)(2,1)S(1)} %slice_bitcast_fusion), channel_id=1, source_target_pairs={{0,16},{4,20},{8,24},{12,28},{16,0},{20,4},{24,8},{28,12},{1,17},{... | collective-permute-start | bytes 442376 | tf_op jit(solution)/shard_map/ppermute | solution.py:620
  16.5 41.3 %all-to-all-start = ((bf16[16,64,512]{2,1,0:T(8,128)(2,1)}), bf16[16,64,512]{2,1,0:T(8,128)(2,1)S(1)}, u32[]{:S(2)}, u32[]{:S(2)}) async-start(bf16[16,64,512]{2,1,0:T(8,128)(2,1)} %param.19), calls=%async_computation | async-start | bytes 2097152 | tf_op jit(solution)/shard_map/all_to_all | solution.py:628
  24.3 20.7 %collective-permute-start.12 = (bf16[2,18,16,256]{3,2,1,0:T(8,128)(2,1)S(1)}, bf16[2,18,16,256]{3,2,1,0:T(8,128)(2,1)S(1)}, u32[]{:S(2)}, u32[]{:S(2)}) collective-permute-start(bf16[2,18,16,256]{3,2,1,0:T(8,128)(2,1)S(1)} %pad_maximum_fusion.12), channel_id=1, source_target_pairs={{0,8},{4,12},{8,0},{12,4},{16,24},{20,28},{24,16},{28,20},{1,9},{5... | collective-permute-start | bytes 884744 | tf_op jit(solution)/shard_map/ppermute | solution.py:620
  25.6 10.3 %collective-permute-start.5 = (bf16[4,4,16,256]{3,2,1,0:T(8,128)(2,1)S(1)}, bf16[4,4,16,256]{3,2,1,0:T(8,128)(2,1)S(1)}, u32[]{:S(2)}, u32[]{:S(2)}) collective-permute-start(bf16[4,4,16,256]{3,2,1,0:T(8,128)(2,1)S(1)} %slice.230), channel_id=1, source_target_pairs={{0,4},{4,0},{8,12},{12,8},{16,20},{20,16},{24,28},{28,24},{1,5},{5... | collective-permute-start | bytes 393224 | tf_op jit(solution)/shard_map/ppermute | solution.py:620
  29.2 19.4 %collective-permute-start.9 = (bf16[8,3,16,256]{3,2,1,0:T(8,128)(2,1)S(1)}, bf16[8,3,16,256]{3,2,1,0:T(8,128)(2,1)S(1)}, u32[]{:S(2)}, u32[]{:S(2)}) collective-permute-start(bf16[8,3,16,256]{3,2,1,0:T(8,128)(2,1)S(1)} %pad_maximum_fusion.17), channel_id=1, source_target_pairs={{0,4},{4,0},{8,12},{12,8},{16,20},{20,16},{24,28},{28,24},{1,5},{5... | collective-permute-start | bytes 589832 | tf_op jit(solution)/shard_map/ppermute | solution.py:620
  36.0 12.7 %collective-permute-start.6 = (bf16[8,4,16,256]{3,2,1,0:T(8,128)(2,1)S(1)}, bf16[8,4,16,256]{3,2,1,0:T(8,128)(2,1)S(1)}, u32[]{:S(2)}, u32[]{:S(2)}) collective-permute-start(bf16[8,4,16,256]{3,2,1,0:T(8,128)(2,1)S(1)} %pad_maximum_fusion.10), channel_id=1, source_target_pairs={{0,2},{1,3},{2,0},{3,1},{4,6},{5,7},{6,4},{7,5},{8,10},{9,11},{10,... | collective-permute-start | bytes 786440 | tf_op jit(solution)/shard_map/ppermute | solution.py:620
  46.4 9.5 %collective-permute-start.13 = (bf16[4,9,16,256]{3,2,1,0:T(8,128)(2,1)S(1)}, bf16[4,9,16,256]{3,2,1,0:T(8,128)(2,1)S(1)}, u32[]{:S(2)}, u32[]{:S(2)}) collective-permute-start(bf16[4,9,16,256]{3,2,1,0:T(8,128)(2,1)S(1)} %get-tuple-element.139), channel_id=1, source_target_pairs={{0,4},{4,0},{8,12},{12,8},{16,20},{20,16},{24,28},{28,24},{1,5},{5... | collective-permute-start | bytes 884744 | tf_op jit(solution)/shard_map/ppermute | solution.py:620
  48.7 17.6 %collective-permute-start.7 = (bf16[16,4,16,256]{3,2,1,0:T(8,128)(2,1)S(1)}, bf16[16,4,16,256]{3,2,1,0:T(8,128)(2,1)}, u32[]{:S(2)}, u32[]{:S(2)}) collective-permute-start(bf16[16,4,16,256]{3,2,1,0:T(8,128)(2,1)S(1)} %pad_maximum_fusion.6.refs_0_), channel_id=1, source_target_pairs={{0,1},{1,0},{2,3},{3,2},{4,5},{5,4},{6,7},{7,6},{8,9},{9,8},{10,11... | collective-permute-start | bytes 1572872 | tf_op jit(solution)/shard_map/ppermute | solution.py:620
  53.8 21.7 %collective-permute-start.16 = (bf16[8,9,16,256]{3,2,1,0:T(8,128)(2,1)}, bf16[8,9,16,256]{3,2,1,0:T(8,128)(2,1)}, u32[]{:S(2)}, u32[]{:S(2)}) collective-permute-start(bf16[8,9,16,256]{3,2,1,0:T(8,128)(2,1)} %pad_maximum_fusion.5), channel_id=1, source_target_pairs={{0,4},{4,0},{8,12},{12,8},{16,20},{20,16},{24,28},{28,24},{1,5},{5... | collective-permute-start | bytes 1769480 | tf_op jit(solution)/shard_map/ppermute | solution.py:620
  56.8 18.6 %collective-permute-start.14 = (bf16[8,9,16,256]{3,2,1,0:T(8,128)(2,1)}, bf16[8,9,16,256]{3,2,1,0:T(8,128)(2,1)}, u32[]{:S(2)}, u32[]{:S(2)}) collective-permute-start(bf16[8,9,16,256]{3,2,1,0:T(8,128)(2,1)} %pad_maximum_fusion.4), channel_id=1, source_target_pairs={{0,2},{1,3},{2,0},{3,1},{4,6},{5,7},{6,4},{7,5},{8,10},{9,11},{10,... | collective-permute-start | bytes 1769480 | tf_op jit(solution)/shard_map/ppermute | solution.py:620
  57.8 33.5 %all-to-all-start.1 = ((bf16[16,64,512]{2,1,0:T(8,128)(2,1)}), bf16[16,64,512]{2,1,0:T(8,128)(2,1)}, u32[]{:S(2)}, u32[]{:S(2)}) async-start(bf16[16,64,512]{2,1,0:T(8,128)(2,1)} %param.20), calls=%async_computation.1 | async-start | bytes 2097152 | tf_op jit(solution)/shard_map/all_to_all | solution.py:628
  119.8 45.5 %all-to-all-start.2 = ((bf16[8,64,1408]{2,1,0:T(8,128)(2,1)}), bf16[8,64,1408]{2,1,0:T(8,128)(2,1)}, u32[]{:S(2)}, u32[]{:S(2)}) async-start(bf16[8,64,1408]{2,1,0:T(8,128)(2,1)} %get-tuple-element.83), calls=%async_computation.2 | async-start | bytes 2883584 | tf_op jit(solution)/shard_map/all_to_all | solution.py:628
  128.0 17.7 %collective-permute-start.20 = (bf16[72,16,256]{2,1,0:T(8,128)(2,1)S(1)}, bf16[72,16,256]{2,1,0:T(8,128)(2,1)S(1)}, u32[]{:S(2)}, u32[]{:S(2)}) collective-permute-start(bf16[72,16,256]{2,1,0:T(8,128)(2,1)S(1)} %get-tuple-element.133), channel_id=1, source_target_pairs={{0,2},{1,3},{2,0},{3,1},{4,6},{5,7},{6,4},{7,5},{8,10},{9,11},{10,... | collective-permute-start | bytes 1769480 | tf_op jit(solution)/shard_map/ppermute | solution.py:620
  128.8 26.5 %collective-permute-start.21 = (bf16[72,16,256]{2,1,0:T(8,128)(2,1)S(1)}, bf16[72,16,256]{2,1,0:T(8,128)(2,1)S(1)}, u32[]{:S(2)}, u32[]{:S(2)}) collective-permute-start(bf16[72,16,256]{2,1,0:T(8,128)(2,1)S(1)} %get-tuple-element.132), channel_id=1, source_target_pairs={{0,4},{4,0},{8,12},{12,8},{16,20},{20,16},{24,28},{28,24},{1,5},{5... | collective-permute-start | bytes 1769480 | tf_op jit(solution)/shard_map/ppermute | solution.py:620
  159.4 15.3 %collective-permute-start.26 = (bf16[24,16,256]{2,1,0:T(8,128)(2,1)S(1)}, bf16[24,16,256]{2,1,0:T(8,128)(2,1)}, u32[]{:S(2)}, u32[]{:S(2)}) collective-permute-start(bf16[24,16,256]{2,1,0:T(8,128)(2,1)S(1)} %slice.252), channel_id=1, source_target_pairs={{0,4},{4,0},{8,12},{12,8},{16,20},{20,16},{24,28},{28,24},{1,5},{5... | collective-permute-start | bytes 589832 | tf_op jit(solution)/shard_map/ppermute | solution.py:620
  159.4 17.5 %collective-permute-start.23 = (bf16[48,16,256]{2,1,0:T(8,128)(2,1)}, bf16[48,16,256]{2,1,0:T(8,128)(2,1)}, u32[]{:S(2)}, u32[]{:S(2)}) collective-permute-start(bf16[48,16,256]{2,1,0:T(8,128)(2,1)} %slice.245), channel_id=1, source_target_pairs={{0,2},{1,3},{2,0},{3,1},{4,6},{5,7},{6,4},{7,5},{8,10},{9,11},{10,... | collective-permute-start | bytes 1179656 | tf_op jit(solution)/shard_map/ppermute | solution.py:620
  161.3 16.7 %collective-permute-start.25 = (bf16[36,16,256]{2,1,0:T(8,128)(2,1)}, bf16[36,16,256]{2,1,0:T(8,128)(2,1)}, u32[]{:S(2)}, u32[]{:S(2)}) collective-permute-start(bf16[36,16,256]{2,1,0:T(8,128)(2,1)} %slice.250), channel_id=1, source_target_pairs={{0,4},{4,0},{8,12},{12,8},{16,20},{20,16},{24,28},{28,24},{1,5},{5... | collective-permute-start | bytes 884744 | tf_op jit(solution)/shard_map/ppermute | solution.py:620
  164.0 15.0 %collective-permute-start.27 = (bf16[36,16,256]{2,1,0:T(8,128)(2,1)}, bf16[36,16,256]{2,1,0:T(8,128)(2,1)}, u32[]{:S(2)}, u32[]{:S(2)}) collective-permute-start(bf16[36,16,256]{2,1,0:T(8,128)(2,1)} %slice.255), channel_id=1, source_target_pairs={{0,2},{1,3},{2,0},{3,1},{4,6},{5,7},{6,4},{7,5},{8,10},{9,11},{10,... | collective-permute-start | bytes 884744 | tf_op jit(solution)/shard_map/ppermute | solution.py:620
  165.3 45.0 %all-to-all-start.3 = ((bf16[16,64,512]{2,1,0:T(8,128)(2,1)}), bf16[16,64,512]{2,1,0:T(8,128)(2,1)S(1)}, u32[]{:S(2)}, u32[]{:S(2)}) async-start(bf16[16,64,512]{2,1,0:T(8,128)(2,1)} %bitcast.20), calls=%async_computation.3 | async-start | bytes 2097152 | tf_op jit(solution)/shard_map/all_to_all | solution.py:628
  182.4 15.8 %collective-permute-start.30 = (bf16[2,18,16,256]{3,2,1,0:T(8,128)(2,1)S(1)}, bf16[2,18,16,256]{3,2,1,0:T(8,128)(2,1)S(1)}, u32[]{:S(2)}, u32[]{:S(2)}) collective-permute-start(bf16[2,18,16,256]{3,2,1,0:T(8,128)(2,1)S(1)} %pad_maximum_fusion.11), channel_id=1, source_target_pairs={{0,8},{4,12},{8,0},{12,4},{16,24},{20,28},{24,16},{28,20},{1,9},{5... | collective-permute-start | bytes 884744 | tf_op jit(solution)/shard_map/ppermute | solution.py:620
  187.9 11.9 %collective-permute-start.29 = (bf16[2,9,16,256]{3,2,1,0:T(8,128)(2,1)S(1)}, bf16[2,9,16,256]{3,2,1,0:T(8,128)(2,1)S(1)}, u32[]{:S(2)}, u32[]{:S(2)}) collective-permute-start(bf16[2,9,16,256]{3,2,1,0:T(8,128)(2,1)S(1)} %fusion.3), channel_id=1, source_target_pairs={{0,8},{4,12},{8,0},{12,4},{16,24},{20,28},{24,16},{28,20},{1,9},{5... | collective-permute-start | bytes 442376 | tf_op jit(solution)/shard_map/ppermute | solution.py:620
  216.3 16.8 %all-to-all-start.4 = ((bf16[8,64,192]{2,1,0:T(8,128)(2,1)}), bf16[8,64,192]{2,1,0:T(8,128)(2,1)S(1)}, u32[]{:S(2)}, u32[]{:S(2)}) async-start(bf16[8,64,192]{2,1,0:T(8,128)(2,1)} %right_turn.1), calls=%async_computation.4 | async-start | bytes 524288 | tf_op jit(solution)/shard_map/all_to_all | solution.py:886
  222.3 10.8 %collective-permute-start.36 = (bf16[1,2,64,256]{3,2,1,0:T(8,128)(2,1)S(1)}, bf16[1,2,64,256]{3,2,1,0:T(8,128)(2,1)S(1)}, u32[]{:S(2)}, u32[]{:S(2)}) collective-permute-start(bf16[1,2,64,256]{3,2,1,0:T(8,128)(2,1)S(1)} %bitcast.103), channel_id=1, source_target_pairs={{0,16},{4,20},{8,24},{12,28},{16,0},{20,4},{24,8},{28,12},{1,17},{... | collective-permute-start | bytes 196616 | tf_op jit(solution)/shard_map/ppermute | solution.py:620
  241.4 14.4 %all-to-all-start.5 = ((bf16[8,64,384]{2,1,0:T(8,128)(2,1)}), bf16[8,64,384]{2,1,0:T(8,128)(2,1)S(1)}, u32[]{:S(2)}, u32[]{:S(2)}) async-start(bf16[8,64,384]{2,1,0:T(8,128)(2,1)} %left_turns.1), calls=%async_computation.5 | async-start | bytes 786432 | tf_op jit(solution)/shard_map/all_to_all | solution.py:888
  (66 other events, 377.1 us)

commit v3 on v2

--- a/solution.py
+++ b/solution.py
@@ -277,8 +277,8 @@
         nt(gpre[:, t * tile : (t + 1) * tile], w_ref[up + t]) for t in range(ups)
     )
     grad_mid, gain_one, shift_one = norm_pull(grad_normed, scaled_one, inverse_one, norm_ref[0:1])
-    mid_ref[0] = grad_mid
     ga = grad_mid.astype(BF)
+    mid_ref[0] = ga
     gmixed_ref[0] = sum(nt(ga[:, t * tile : (t + 1) * tile], w_ref[t]) for t in range(outs)).astype(BF)
     dnorm_ref[...] += jnp.concatenate([gain_one, shift_one, gain_two, shift_two], axis=0)
     for b in range(blocks):
@@ -322,7 +322,7 @@
         + [whole(shape) for shape in grad_shapes],
         out_shape=[
             jax.ShapeDtypeStruct(sent, BF),
-            jax.ShapeDtypeStruct((wins, win, width), F32),
+            jax.ShapeDtypeStruct((wins, win, width), BF),
             jax.ShapeDtypeStruct((wins, win, width), BF),
             jax.ShapeDtypeStruct(norms.shape, F32),
         ]
@@ -428,7 +428,7 @@
             gproj[:, 3 * dim * (h - 1) : 3 * dim * (h + 1)] = jnp.concatenate(parts, axis=1)
     hidden = x_ref[...].reshape(win, width).astype(F32) + pos_ref[...]
     low_t = hidden.astype(BF).T
-    total = mid_ref[0]
+    total = mid_ref[0].astype(F32)
     for t in range(tiles):
         part = gproj[:, t * tile : (t + 1) * tile]
         acc[t] += nn(low_t, part)

time: 258 us -> 258 us (level)
  no operation moved by 1% of the time
where the time goes in v3:
time: 258 us; the launch traced here: 257 us
  waiting for transfers between devices  78.5 us (30%)
  starting transfers between devices  73.9 us (29%)
  Pallas kernels  65.8 us (26%)
  other arithmetic  22.1 us (9%)
  local copies, waits for them, and re-layouts  15.1 us (6%)
    ppermute x39, waiting for transfers between devices, swap(): return lax.ppermute(x, axis, [(i, i ^ bit) for i in range(size)])  65.2 us
    ppermute x39, starting transfers between devices, swap(): return lax.ppermute(x, axis, [(i, i ^ bit) for i in range(size)])  44.2 us
    pallas_call x1, Pallas kernels, middle(): pl.pallas_call(functools.partial(middle_kernel, plans, out_plans, reps, r...  28.3 us
    all_to_all x4, starting transfers between devices, exchange(): return lax.all_to_all(x, axis, 0, 0, axis_index_groups=groups, tiled=True)  21.6 us
    pallas_call x1, Pallas kernels, attend_backward(): pl.pallas_call(functools.partial(attend_back_kernel, plans, out_plans, re...  14.8 us
    all_to_all x4, waiting for transfers between devices, exchange(): return lax.all_to_all(x, axis, 0, 0, axis_index_groups=groups, tiled=True)  9.54 us
    convert_element_type x13, other arithmetic, add(): return (a.astype(F32) + b.astype(F32)).astype(BF)  8.35 us
    pallas_call x1, Pallas kernels, attend_forward(): pl.pallas_call(functools.partial(attend_kernel, plans, reps), grid=(wins,...  7.45 us
  transfers between devices with their start and end apart: 45, of which 24 were waited for; matrix products, arithmetic and copies ran while one was open for 11% of the time, Pallas kernels for 14%

profile of v3, /device:TPU:0, one launch (start us, length us, event | category | flops | bytes accessed | tf_op | source)
XLA Modules:
  0.0 257.0 jit_solution(11535795404079019229)
XLA Ops:
  16.5 5.3 %all-to-all-start = ((bf16[16,64,512]{2,1,0:T(8,128)(2,1)}), bf16[16,64,512]{2,1,0:T(8,128)(2,1)S(1)}, u32[]{:S(2)}, u32[]{:S(2)}) async-start(bf16[16,64,512]{2,1,0:T(8,128)(2,1)} %param.19), calls=%async_computation | async-start | bytes 2097152 | tf_op jit(solution)/shard_map/all_to_all | solution.py:628
  30.7 5.2 %collective-permute-done.5 = bf16[4,4,16,256]{3,2,1,0:T(8,128)(2,1)S(1)} collective-permute-done((bf16[4,4,16,256]{3,2,1,0:T(8,128)(2,1)S(1)}, bf16[4,4,16,256]{3,2,1,0:T(8,128)(2,1)S(1)}, u32[]{:S(2)}, u32[]{:S(2)}) %collective-permute-start.5) | collective-permute-done | bytes 131104 | tf_op jit(solution)/shard_map/ppermute | solution.py:620
  37.1 7.9 %collective-permute-done.12 = bf16[2,18,16,256]{3,2,1,0:T(8,128)(2,1)S(1)} collective-permute-done((bf16[2,18,16,256]{3,2,1,0:T(8,128)(2,1)S(1)}, bf16[2,18,16,256]{3,2,1,0:T(8,128)(2,1)S(1)}, u32[]{:S(2)}, u32[]{:S(2)}) %collective-permute-start.12) | collective-permute-done | bytes 294944 | tf_op jit(solution)/shard_map/ppermute | solution.py:620
  48.8 4.1 %collective-permute-done.15 = bf16[4,9,16,256]{3,2,1,0:T(8,128)(2,1)S(1)} collective-permute-done((bf16[4,9,16,256]{3,2,1,0:T(8,128)(2,1)S(1)}, bf16[4,9,16,256]{3,2,1,0:T(8,128)(2,1)S(1)}, u32[]{:S(2)}, u32[]{:S(2)}) %collective-permute-start.15) | collective-permute-done | bytes 294944 | tf_op jit(solution)/shard_map/ppermute | solution.py:620
  57.8 7.1 %all-to-all-start.1 = ((bf16[16,64,512]{2,1,0:T(8,128)(2,1)}), bf16[16,64,512]{2,1,0:T(8,128)(2,1)}, u32[]{:S(2)}, u32[]{:S(2)}) async-start(bf16[16,64,512]{2,1,0:T(8,128)(2,1)} %param.20), calls=%async_computation.1 | async-start | bytes 2097152 | tf_op jit(solution)/shard_map/all_to_all | solution.py:628
  66.3 7.5 %attend_forward.1 = (bf16[2,512,1536]{2,1,0:T(8,128)(2,1)S(1)}, bf16[2,512,512]{2,1,0:T(8,128)(2,1)S(1)}, f32[2,8,512]{2,1,0:T(8,128)S(1)}) custom-call(s32[2]{0:T(128)S(1)} %pad_add_fusion.me_ref, bf16[8,2,64,512]{3,2,1,0:T(8,128)(2,1)S(1)} %bitcast.85, f32[512,512]{1,0:T(8,128)S(1)} %copy-done, s32[2,1,512]{2,1,0:T(1,128)S(1)} %broadcast_in_dim_reshape.8.ids_row, ...), custom_call_target="tpu_custom_call" | custom-call | flops 18000000 | tf_op jit(solution)/shard_map/attend_forward/pallas_call | solution.py:184
  81.8 9.5 %all-to-all-done.1 = bf16[16,64,512]{2,1,0:T(8,128)(2,1)} async-done(((bf16[16,64,512]{2,1,0:T(8,128)(2,1)}), bf16[16,64,512]{2,1,0:T(8,128)(2,1)}, u32[]{:S(2)}, u32[]{:S(2)}) %all-to-all-start.1) | async-done | bytes 1048608 | tf_op jit(solution)/shard_map/all_to_all | solution.py:628
  91.3 28.3 %middle.1 = (bf16[8,64,1408]{2,1,0:T(8,128)(2,1)}, bf16[2,512,512]{2,1,0:T(8,128)(2,1)}, bf16[2,512,512]{2,1,0:T(8,128)(2,1)}, f32[4,512]{1,0:T(4,128)}, bf16[28...) custom-call(s32[2]{0:T(128)} %copy-done.16, bf16[8,2,64,512]{3,2,1,0:T(8,128)(2,1)} %bitcast.86, ...), custom_call_target="tpu_custom_call" | custom-call | flops 27000000 | tf_op jit(solution)/shard_map/middle/pallas_call | solution.py:308
  119.7 4.5 %all-to-all-start.2 = ((bf16[8,64,1408]{2,1,0:T(8,128)(2,1)}), bf16[8,64,1408]{2,1,0:T(8,128)(2,1)}, u32[]{:S(2)}, u32[]{:S(2)}) async-start(bf16[8,64,1408]{2,1,0:T(8,128)(2,1)} %get-tuple-element.83), calls=%async_computation.2 | async-start | bytes 2883584 | tf_op jit(solution)/shard_map/all_to_all | solution.py:628
  124.6 3.1 %add_convert_fusion = bf16[288,16,256]{2,1,0:T(8,128)(2,1)S(1)} fusion(bf16[288,16,256]{2,1,0:T(8,128)(2,1)} %collective-permute-done.19, bf16[288,16,256]{2,1,0:T(8,128)(2,1)} %get-tuple-element.89), kind=kLoop, calls=%fused_computation.7 | loop fusion | flops 4718592 | bytes 7077888 | tf_op jit(solution)/shard_map/convert_element_type | solution.py:653
  130.7 14.8 %attend_backward.1 = (bf16[8,2,64,512]{3,2,1,0:T(8,128)(2,1)}, bf16[144,16,256]{2,1,0:T(8,128)(2,1)S(1)}, bf16[144,16,256]{2,1,0:T(8,128)(2,1)S(1)}) custom-call(s32[2]{0:T(128)S(1)} %copy-done.17, bf16[8,2,64,512]{3,2,1,0:T(8,128)(2,1)S(1)} %bitcast.87, f32[512,512]{1,0:T(8,128)S(1)} %copy-done.1, s32[2,1,512]{2,1,0:T(1,128)S(1)} %broadcast_in_dim_reshape.8.ids_row, ...), custom_call_target="tpu_custom_call" | custom-call | flops 22000000 | tf_op jit(solution)/shard_map/attend_backward/pallas_call | solution.py:459
  145.5 9.7 %collective-permute-done.21 = bf16[72,16,256]{2,1,0:T(8,128)(2,1)S(1)} collective-permute-done((bf16[72,16,256]{2,1,0:T(8,128)(2,1)S(1)}, bf16[72,16,256]{2,1,0:T(8,128)(2,1)S(1)}, u32[]{:S(2)}, u32[]{:S(2)}) %collective-permute-start.21) | collective-permute-done | bytes 589856 | tf_op jit(solution)/shard_map/ppermute | solution.py:620
  165.2 4.6 %all-to-all-start.3 = ((bf16[16,64,512]{2,1,0:T(8,128)(2,1)}), bf16[16,64,512]{2,1,0:T(8,128)(2,1)S(1)}, u32[]{:S(2)}, u32[]{:S(2)}) async-start(bf16[16,64,512]{2,1,0:T(8,128)(2,1)} %bitcast.20), calls=%async_computation.3 | async-start | bytes 2097152 | tf_op jit(solution)/shard_map/all_to_all | solution.py:628
  169.8 4.7 %low_bases.1 = (bf16[6,512,512]{2,1,0:T(8,128)(2,1)}, bf16[6,256,256]{2,1,0:T(8,128)(2,1)}) custom-call(f32[6,512,512]{2,1,0:T(8,128)} %left_ref, f32[6,256,256]{2,1,0:T(8,128)} %right_ref.1), custom_call_target="tpu_custom_call" | custom-call | flops 3000000 | tf_op jit(solution)/shard_map/low_bases/pallas_call | solution.py:603
  183.9 3.8 %collective-permute-done.24 = bf16[24,16,256]{2,1,0:T(8,128)(2,1)S(1)} collective-permute-done((bf16[24,16,256]{2,1,0:T(8,128)(2,1)S(1)}, bf16[24,16,256]{2,1,0:T(8,128)(2,1)S(1)}, u32[]{:S(2)}, u32[]{:S(2)}) %collective-permute-start.24) | collective-permute-done | bytes 196640 | tf_op jit(solution)/shard_map/ppermute | solution.py:620
  187.8 3.4 %collective-permute-start.29 = (bf16[2,9,16,256]{3,2,1,0:T(8,128)(2,1)S(1)}, bf16[2,9,16,256]{3,2,1,0:T(8,128)(2,1)S(1)}, u32[]{:S(2)}, u32[]{:S(2)}) collective-permute-start(bf16[2,9,16,256]{3,2,1,0:T(8,128)(2,1)S(1)} %fusion.3), channel_id=1, source_target_pairs={{0,8},{4,12},{8,0},{12,4},{16,24},{20,28},{24,16},{28,20},{1,9},{5... | collective-permute-start | bytes 442376 | tf_op jit(solution)/shard_map/ppermute | solution.py:620
  191.2 6.8 %collective-permute-done.30 = bf16[2,18,16,256]{3,2,1,0:T(8,128)(2,1)S(1)} collective-permute-done((bf16[2,18,16,256]{3,2,1,0:T(8,128)(2,1)S(1)}, bf16[2,18,16,256]{3,2,1,0:T(8,128)(2,1)S(1)}, u32[]{:S(2)}, u32[]{:S(2)}) %collective-permute-start.30) | collective-permute-done | bytes 294944 | tf_op jit(solution)/shard_map/ppermute | solution.py:620
  201.9 4.7 %collective-permute-done.32 = bf16[1,18,16,256]{3,2,1,0:T(8,128)(2,1)S(1)} collective-permute-done((bf16[1,18,16,256]{3,2,1,0:T(8,128)(2,1)S(1)}, bf16[1,18,16,256]{3,2,1,0:T(8,128)(2,1)S(1)}, u32[]{:S(2)}, u32[]{:S(2)}) %collective-permute-start.32) | collective-permute-done | bytes 147488 | tf_op jit(solution)/shard_map/ppermute | solution.py:620
  216.2 4.6 %all-to-all-start.4 = ((bf16[8,64,192]{2,1,0:T(8,128)(2,1)}), bf16[8,64,192]{2,1,0:T(8,128)(2,1)S(1)}, u32[]{:S(2)}, u32[]{:S(2)}) async-start(bf16[8,64,192]{2,1,0:T(8,128)(2,1)} %right_turn.1), calls=%async_computation.4 | async-start | bytes 524288 | tf_op jit(solution)/shard_map/all_to_all | solution.py:886
  222.1 3.0 %collective-permute-start.36 = (bf16[1,2,64,256]{3,2,1,0:T(8,128)(2,1)S(1)}, bf16[1,2,64,256]{3,2,1,0:T(8,128)(2,1)S(1)}, u32[]{:S(2)}, u32[]{:S(2)}) collective-permute-start(bf16[1,2,64,256]{3,2,1,0:T(8,128)(2,1)S(1)} %bitcast.103), channel_id=1, source_target_pairs={{0,16},{4,20},{8,24},{12,28},{16,0},{20,4},{24,8},{28,12},{1,17},{... | collective-permute-start | bytes 196616 | tf_op jit(solution)/shard_map/ppermute | solution.py:620
  226.1 6.8 %collective-permute-done.36 = bf16[1,2,64,256]{3,2,1,0:T(8,128)(2,1)S(1)} collective-permute-done((bf16[1,2,64,256]{3,2,1,0:T(8,128)(2,1)S(1)}, bf16[1,2,64,256]{3,2,1,0:T(8,128)(2,1)S(1)}, u32[]{:S(2)}, u32[]{:S(2)}) %collective-permute-start.36) | collective-permute-done | bytes 65568 | tf_op jit(solution)/shard_map/ppermute | solution.py:620
  233.6 5.4 %left_turns.1 = bf16[8,64,384]{2,1,0:T(8,128)(2,1)} custom-call(bf16[8,64,192]{2,1,0:T(8,128)(2,1)} %copy-done.36, bf16[8,64,1408]{2,1,0:T(8,128)(2,1)} %all-to-all-done.2.moments_ref, bf16[6,512,512]{2,1,0:T(8,128)(2,1)} %get-tuple-element.99.left_ref), custom_call_target="tpu_custom_call" | custom-call | flops 3000000 | tf_op jit(solution)/shard_map/left_turns/pallas_call | solution.py:531
  241.2 3.5 %all-to-all-start.5 = ((bf16[8,64,384]{2,1,0:T(8,128)(2,1)}), bf16[8,64,384]{2,1,0:T(8,128)(2,1)S(1)}, u32[]{:S(2)}, u32[]{:S(2)}) async-start(bf16[8,64,384]{2,1,0:T(8,128)(2,1)} %left_turns.1), calls=%async_computation.5 | async-start | bytes 786432 | tf_op jit(solution)/shard_map/all_to_all | solution.py:888
  251.9 3.7 %all-to-all-done.5.back_ref = bf16[8,64,384]{2,1,0:T(8,128)(2,1)S(1)} async-done(((bf16[8,64,384]{2,1,0:T(8,128)(2,1)}), bf16[8,64,384]{2,1,0:T(8,128)(2,1)S(1)}, u32[]{:S(2)}, u32[]{:S(2)}) %all-to-all-start.5) | async-done | bytes 393248 | tf_op jit(solution)/shard_map/all_to_all | solution.py:888
  (275 shorter events, 93.4 us)
Async XLA Ops:
  14.5 9.8 %collective-permute-start.11 = (bf16[1,18,16,256]{3,2,1,0:T(8,128)(2,1)S(1)}, bf16[1,18,16,256]{3,2,1,0:T(8,128)(2,1)S(1)}, u32[]{:S(2)}, u32[]{:S(2)}) collective-permute-start(bf16[1,18,16,256]{3,2,1,0:T(8,128)(2,1)S(1)} %slice_bitcast_fusion), channel_id=1, source_target_pairs={{0,16},{4,20},{8,24},{12,28},{16,0},{20,4},{24,8},{28,12},{1,17},{... | collective-permute-start | bytes 442376 | tf_op jit(solution)/shard_map/ppermute | solution.py:620
  16.5 41.3 %all-to-all-start = ((bf16[16,64,512]{2,1,0:T(8,128)(2,1)}), bf16[16,64,512]{2,1,0:T(8,128)(2,1)S(1)}, u32[]{:S(2)}, u32[]{:S(2)}) async-start(bf16[16,64,512]{2,1,0:T(8,128)(2,1)} %param.19), calls=%async_computation | async-start | bytes 2097152 | tf_op jit(solution)/shard_map/all_to_all | solution.py:628
  24.3 20.7 %collective-permute-start.12 = (bf16[2,18,16,256]{3,2,1,0:T(8,128)(2,1)S(1)}, bf16[2,18,16,256]{3,2,1,0:T(8,128)(2,1)S(1)}, u32[]{:S(2)}, u32[]{:S(2)}) collective-permute-start(bf16[2,18,16,256]{3,2,1,0:T(8,128)(2,1)S(1)} %pad_maximum_fusion.12), channel_id=1, source_target_pairs={{0,8},{4,12},{8,0},{12,4},{16,24},{20,28},{24,16},{28,20},{1,9},{5... | collective-permute-start | bytes 884744 | tf_op jit(solution)/shard_map/ppermute | solution.py:620
  25.6 10.3 %collective-permute-start.5 = (bf16[4,4,16,256]{3,2,1,0:T(8,128)(2,1)S(1)}, bf16[4,4,16,256]{3,2,1,0:T(8,128)(2,1)S(1)}, u32[]{:S(2)}, u32[]{:S(2)}) collective-permute-start(bf16[4,4,16,256]{3,2,1,0:T(8,128)(2,1)S(1)} %slice.230), channel_id=1, source_target_pairs={{0,4},{4,0},{8,12},{12,8},{16,20},{20,16},{24,28},{28,24},{1,5},{5... | collective-permute-start | bytes 393224 | tf_op jit(solution)/shard_map/ppermute | solution.py:620
  29.2 19.4 %collective-permute-start.9 = (bf16[8,3,16,256]{3,2,1,0:T(8,128)(2,1)S(1)}, bf16[8,3,16,256]{3,2,1,0:T(8,128)(2,1)S(1)}, u32[]{:S(2)}, u32[]{:S(2)}) collective-permute-start(bf16[8,3,16,256]{3,2,1,0:T(8,128)(2,1)S(1)} %pad_maximum_fusion.17), channel_id=1, source_target_pairs={{0,4},{4,0},{8,12},{12,8},{16,20},{20,16},{24,28},{28,24},{1,5},{5... | collective-permute-start | bytes 589832 | tf_op jit(solution)/shard_map/ppermute | solution.py:620
  36.0 12.7 %collective-permute-start.6 = (bf16[8,4,16,256]{3,2,1,0:T(8,128)(2,1)S(1)}, bf16[8,4,16,256]{3,2,1,0:T(8,128)(2,1)S(1)}, u32[]{:S(2)}, u32[]{:S(2)}) collective-permute-start(bf16[8,4,16,256]{3,2,1,0:T(8,128)(2,1)S(1)} %pad_maximum_fusion.10), channel_id=1, source_target_pairs={{0,2},{1,3},{2,0},{3,1},{4,6},{5,7},{6,4},{7,5},{8,10},{9,11},{10,... | collective-permute-start | bytes 786440 | tf_op jit(solution)/shard_map/ppermute | solution.py:620
  46.4 9.5 %collective-permute-start.13 = (bf16[4,9,16,256]{3,2,1,0:T(8,128)(2,1)S(1)}, bf16[4,9,16,256]{3,2,1,0:T(8,128)(2,1)S(1)}, u32[]{:S(2)}, u32[]{:S(2)}) collective-permute-start(bf16[4,9,16,256]{3,2,1,0:T(8,128)(2,1)S(1)} %get-tuple-element.139), channel_id=1, source_target_pairs={{0,4},{4,0},{8,12},{12,8},{16,20},{20,16},{24,28},{28,24},{1,5},{5... | collective-permute-start | bytes 884744 | tf_op jit(solution)/shard_map/ppermute | solution.py:620
  48.7 17.6 %collective-permute-start.7 = (bf16[16,4,16,256]{3,2,1,0:T(8,128)(2,1)S(1)}, bf16[16,4,16,256]{3,2,1,0:T(8,128)(2,1)}, u32[]{:S(2)}, u32[]{:S(2)}) collective-permute-start(bf16[16,4,16,256]{3,2,1,0:T(8,128)(2,1)S(1)} %pad_maximum_fusion.6.refs_0_), channel_id=1, source_target_pairs={{0,1},{1,0},{2,3},{3,2},{4,5},{5,4},{6,7},{7,6},{8,9},{9,8},{10,11... | collective-permute-start | bytes 1572872 | tf_op jit(solution)/shard_map/ppermute | solution.py:620
  53.8 21.7 %collective-permute-start.16 = (bf16[8,9,16,256]{3,2,1,0:T(8,128)(2,1)}, bf16[8,9,16,256]{3,2,1,0:T(8,128)(2,1)}, u32[]{:S(2)}, u32[]{:S(2)}) collective-permute-start(bf16[8,9,16,256]{3,2,1,0:T(8,128)(2,1)} %pad_maximum_fusion.5), channel_id=1, source_target_pairs={{0,4},{4,0},{8,12},{12,8},{16,20},{20,16},{24,28},{28,24},{1,5},{5... | collective-permute-start | bytes 1769480 | tf_op jit(solution)/shard_map/ppermute | solution.py:620
  56.8 18.6 %collective-permute-start.14 = (bf16[8,9,16,256]{3,2,1,0:T(8,128)(2,1)}, bf16[8,9,16,256]{3,2,1,0:T(8,128)(2,1)}, u32[]{:S(2)}, u32[]{:S(2)}) collective-permute-start(bf16[8,9,16,256]{3,2,1,0:T(8,128)(2,1)} %pad_maximum_fusion.4), channel_id=1, source_target_pairs={{0,2},{1,3},{2,0},{3,1},{4,6},{5,7},{6,4},{7,5},{8,10},{9,11},{10,... | collective-permute-start | bytes 1769480 | tf_op jit(solution)/shard_map/ppermute | solution.py:620
  57.8 33.5 %all-to-all-start.1 = ((bf16[16,64,512]{2,1,0:T(8,128)(2,1)}), bf16[16,64,512]{2,1,0:T(8,128)(2,1)}, u32[]{:S(2)}, u32[]{:S(2)}) async-start(bf16[16,64,512]{2,1,0:T(8,128)(2,1)} %param.20), calls=%async_computation.1 | async-start | bytes 2097152 | tf_op jit(solution)/shard_map/all_to_all | solution.py:628
  119.7 45.5 %all-to-all-start.2 = ((bf16[8,64,1408]{2,1,0:T(8,128)(2,1)}), bf16[8,64,1408]{2,1,0:T(8,128)(2,1)}, u32[]{:S(2)}, u32[]{:S(2)}) async-start(bf16[8,64,1408]{2,1,0:T(8,128)(2,1)} %get-tuple-element.83), calls=%async_computation.2 | async-start | bytes 2883584 | tf_op jit(solution)/shard_map/all_to_all | solution.py:628
  127.8 17.7 %collective-permute-start.20 = (bf16[72,16,256]{2,1,0:T(8,128)(2,1)S(1)}, bf16[72,16,256]{2,1,0:T(8,128)(2,1)S(1)}, u32[]{:S(2)}, u32[]{:S(2)}) collective-permute-start(bf16[72,16,256]{2,1,0:T(8,128)(2,1)S(1)} %get-tuple-element.133), channel_id=1, source_target_pairs={{0,2},{1,3},{2,0},{3,1},{4,6},{5,7},{6,4},{7,5},{8,10},{9,11},{10,... | collective-permute-start | bytes 1769480 | tf_op jit(solution)/shard_map/ppermute | solution.py:620
  128.6 26.6 %collective-permute-start.21 = (bf16[72,16,256]{2,1,0:T(8,128)(2,1)S(1)}, bf16[72,16,256]{2,1,0:T(8,128)(2,1)S(1)}, u32[]{:S(2)}, u32[]{:S(2)}) collective-permute-start(bf16[72,16,256]{2,1,0:T(8,128)(2,1)S(1)} %get-tuple-element.132), channel_id=1, source_target_pairs={{0,4},{4,0},{8,12},{12,8},{16,20},{20,16},{24,28},{28,24},{1,5},{5... | collective-permute-start | bytes 1769480 | tf_op jit(solution)/shard_map/ppermute | solution.py:620
  159.2 15.3 %collective-permute-start.26 = (bf16[24,16,256]{2,1,0:T(8,128)(2,1)S(1)}, bf16[24,16,256]{2,1,0:T(8,128)(2,1)}, u32[]{:S(2)}, u32[]{:S(2)}) collective-permute-start(bf16[24,16,256]{2,1,0:T(8,128)(2,1)S(1)} %slice.252), channel_id=1, source_target_pairs={{0,4},{4,0},{8,12},{12,8},{16,20},{20,16},{24,28},{28,24},{1,5},{5... | collective-permute-start | bytes 589832 | tf_op jit(solution)/shard_map/ppermute | solution.py:620
  159.2 17.4 %collective-permute-start.23 = (bf16[48,16,256]{2,1,0:T(8,128)(2,1)}, bf16[48,16,256]{2,1,0:T(8,128)(2,1)}, u32[]{:S(2)}, u32[]{:S(2)}) collective-permute-start(bf16[48,16,256]{2,1,0:T(8,128)(2,1)} %slice.245), channel_id=1, source_target_pairs={{0,2},{1,3},{2,0},{3,1},{4,6},{5,7},{6,4},{7,5},{8,10},{9,11},{10,... | collective-permute-start | bytes 1179656 | tf_op jit(solution)/shard_map/ppermute | solution.py:620
  161.2 16.6 %collective-permute-start.25 = (bf16[36,16,256]{2,1,0:T(8,128)(2,1)}, bf16[36,16,256]{2,1,0:T(8,128)(2,1)}, u32[]{:S(2)}, u32[]{:S(2)}) collective-permute-start(bf16[36,16,256]{2,1,0:T(8,128)(2,1)} %slice.250), channel_id=1, source_target_pairs={{0,4},{4,0},{8,12},{12,8},{16,20},{20,16},{24,28},{28,24},{1,5},{5... | collective-permute-start | bytes 884744 | tf_op jit(solution)/shard_map/ppermute | solution.py:620
  163.9 15.0 %collective-permute-start.27 = (bf16[36,16,256]{2,1,0:T(8,128)(2,1)}, bf16[36,16,256]{2,1,0:T(8,128)(2,1)}, u32[]{:S(2)}, u32[]{:S(2)}) collective-permute-start(bf16[36,16,256]{2,1,0:T(8,128)(2,1)} %slice.255), channel_id=1, source_target_pairs={{0,2},{1,3},{2,0},{3,1},{4,6},{5,7},{6,4},{7,5},{8,10},{9,11},{10,... | collective-permute-start | bytes 884744 | tf_op jit(solution)/shard_map/ppermute | solution.py:620
  165.2 45.0 %all-to-all-start.3 = ((bf16[16,64,512]{2,1,0:T(8,128)(2,1)}), bf16[16,64,512]{2,1,0:T(8,128)(2,1)S(1)}, u32[]{:S(2)}, u32[]{:S(2)}) async-start(bf16[16,64,512]{2,1,0:T(8,128)(2,1)} %bitcast.20), calls=%async_computation.3 | async-start | bytes 2097152 | tf_op jit(solution)/shard_map/all_to_all | solution.py:628
  182.3 15.7 %collective-permute-start.30 = (bf16[2,18,16,256]{3,2,1,0:T(8,128)(2,1)S(1)}, bf16[2,18,16,256]{3,2,1,0:T(8,128)(2,1)S(1)}, u32[]{:S(2)}, u32[]{:S(2)}) collective-permute-start(bf16[2,18,16,256]{3,2,1,0:T(8,128)(2,1)S(1)} %pad_maximum_fusion.11), channel_id=1, source_target_pairs={{0,8},{4,12},{8,0},{12,4},{16,24},{20,28},{24,16},{28,20},{1,9},{5... | collective-permute-start | bytes 884744 | tf_op jit(solution)/shard_map/ppermute | solution.py:620
  187.8 11.8 %collective-permute-start.29 = (bf16[2,9,16,256]{3,2,1,0:T(8,128)(2,1)S(1)}, bf16[2,9,16,256]{3,2,1,0:T(8,128)(2,1)S(1)}, u32[]{:S(2)}, u32[]{:S(2)}) collective-permute-start(bf16[2,9,16,256]{3,2,1,0:T(8,128)(2,1)S(1)} %fusion.3), channel_id=1, source_target_pairs={{0,8},{4,12},{8,0},{12,4},{16,24},{20,28},{24,16},{28,20},{1,9},{5... | collective-permute-start | bytes 442376 | tf_op jit(solution)/shard_map/ppermute | solution.py:620
  216.2 16.7 %all-to-all-start.4 = ((bf16[8,64,192]{2,1,0:T(8,128)(2,1)}), bf16[8,64,192]{2,1,0:T(8,128)(2,1)S(1)}, u32[]{:S(2)}, u32[]{:S(2)}) async-start(bf16[8,64,192]{2,1,0:T(8,128)(2,1)} %right_turn.1), calls=%async_computation.4 | async-start | bytes 524288 | tf_op jit(solution)/shard_map/all_to_all | solution.py:886
  222.1 10.8 %collective-permute-start.36 = (bf16[1,2,64,256]{3,2,1,0:T(8,128)(2,1)S(1)}, bf16[1,2,64,256]{3,2,1,0:T(8,128)(2,1)S(1)}, u32[]{:S(2)}, u32[]{:S(2)}) collective-permute-start(bf16[1,2,64,256]{3,2,1,0:T(8,128)(2,1)S(1)} %bitcast.103), channel_id=1, source_target_pairs={{0,16},{4,20},{8,24},{12,28},{16,0},{20,4},{24,8},{28,12},{1,17},{... | collective-permute-start | bytes 196616 | tf_op jit(solution)/shard_map/ppermute | solution.py:620
  241.2 14.4 %all-to-all-start.5 = ((bf16[8,64,384]{2,1,0:T(8,128)(2,1)}), bf16[8,64,384]{2,1,0:T(8,128)(2,1)S(1)}, u32[]{:S(2)}, u32[]{:S(2)}) async-start(bf16[8,64,384]{2,1,0:T(8,128)(2,1)} %left_turns.1), calls=%async_computation.5 | async-start | bytes 786432 | tf_op jit(solution)/shard_map/all_to_all | solution.py:888
  (66 other events, 376.8 us)
